TPU v7x, 256 devices: a whole 4x4x8 slice. The times are simulated.
256 devices in a mesh: seq: 64 (over z, y, core), dp: 4 (over x).
Axes of the slice: x: 4, y: 4, z: 8, core: 2. Of those that a mesh axis runs over, the one named last changes fastest.
Arguments:
- queries: bfloat16 [4, 32768, 1024], P('dp', 'seq'), may hold values from -8 to 8
- memory_keys: bfloat16 [4, 32768, 1024], P('dp', 'seq'), may hold values from -8 to 8
- memory_values: bfloat16 [4, 32768, 1024], P('dp', 'seq'), may hold values from -6 to 6
- out_weight: bfloat16 [1024, 2048], P('seq'), may hold values from -0.1875 to 0.1875
- grad_out: bfloat16 [4, 32768, 2048], P('dp', 'seq'), may hold values from -6 to 6
- key_first: int32 [4, 256], P('dp', 'seq'), may hold values from 0 to 254, as said below
- key_last: int32 [4, 256], P('dp', 'seq'), may hold values from 2 to 256
Outputs:
- layer_out: bfloat16 [4, 32768, 2048], P('dp', 'seq')
- grad_query: bfloat16 [4, 32768, 1024], P('dp', 'seq')
- grad_keys: bfloat16 [4, 32768, 1024], P('dp', 'seq')
- grad_values: bfloat16 [4, 32768, 1024], P('dp', 'seq')
- weight_grad: float32 [1024, 2048], P('seq')
Inputs may be any that keep to these rules, and one draw needn't show every extreme that they name: With key_last: query block b of pack p attends to key blocks key_first[p, b] to key_last[p, b] - 1, blocks of 128 tokens. Sentence pairs tile aligned groups of 4 blocks that begin at block 2, the first and last groups holding 4 // 2 blocks; a query block's key blocks lie in its own group and number 1 to 3, 3 in some group of every pack.
All inputs are finite; a program needn't handle non-finite values.
Results may differ from a plain program's by a relative error of at most 0.0095.
Values may be sent and summed in bfloat16 or wider, within the bound.
A program may use at most 192 MiB of HBM per device.

v0:
```python
import math

import jax
import jax.numpy as jnp
from jax import lax
from jax.sharding import PartitionSpec as P

HDIM = 128
HEADS = 8
BLOCK = 128
REACH = 256


def padded_2(block, sides, width):
    for axis, dim in sides:
        count = lax.axis_size(axis)
        forward = [(i, i + 1) for i in range(count - 1)]
        backward = [(target, source) for source, target in forward]
        low = lax.ppermute(
            lax.slice_in_dim(block, block.shape[dim] - width, None, axis=dim), axis, forward
        )
        high = lax.ppermute(lax.slice_in_dim(block, 0, width, axis=dim), axis, backward)
        block = jnp.concatenate([low, block, high], axis=dim)
    return block


def passed_along(block, axis, distance):
    devices = range(lax.axis_size(axis))
    route = [(i - distance, i) for i in devices if i - distance in devices]
    return lax.ppermute(block, axis, route)


def run_tiles(
    query_rows, grad_rows, kv_source, window_starts, window_rows, lower, upper, row_anchor
):
    rows_dev, width_hd = query_rows.shape
    set_count = rows_dev // BLOCK // 4
    score_scale = 1.0 / math.sqrt(HDIM)

    def advance(running, set_index):
        member_ids = set_index * 4 + jnp.arange(4, dtype=jnp.int32)
        query_set = query_rows.reshape(4, BLOCK, HEADS, HDIM)
        grad_set = grad_rows.reshape(4, BLOCK, HEADS, HDIM)
        starts = window_starts[member_ids]
        kv_tiles = jax.vmap(
            lambda offset: lax.dynamic_slice_in_dim(kv_source, offset, window_rows, 1)
        )(starts)
        key_tiles = kv_tiles[:, 0].reshape(4, window_rows, HEADS, HDIM)
        value_tiles = kv_tiles[:, 1].reshape(4, window_rows, HEADS, HDIM)
        positions = (
            row_anchor + starts[:, None] + jnp.arange(window_rows, dtype=jnp.int32)[None, :]
        ) // BLOCK
        allowed = (positions >= lower[member_ids][:, None]) & (
            positions < upper[member_ids][:, None]
        )
        inside = allowed[:, None, None, :]
        scores = (
            jnp.einsum("jqhd,jkhd->jhqk", query_set, key_tiles, preferred_element_type=jnp.float32)
            * score_scale
        )
        highest = jnp.max(jnp.where(inside, scores, -jnp.inf), axis=-1, keepdims=True)
        raised = jnp.where(inside, jnp.exp(scores - highest), 0.0)
        softmax_probs = raised / jnp.sum(raised, axis=-1, keepdims=True)
        weights = softmax_probs.astype(jnp.bfloat16)
        attended = jnp.einsum(
            "jhqk,jkhd->jqhd", weights, value_tiles, preferred_element_type=jnp.float32
        ).astype(jnp.bfloat16)
        grad_probs = jnp.einsum(
            "jqhd,jkhd->jhqk", grad_set, value_tiles, preferred_element_type=jnp.float32
        )
        row_term = jnp.sum(softmax_probs * grad_probs, axis=-1, keepdims=True)
        grad_scores = (softmax_probs * (grad_probs - row_term) * score_scale).astype(jnp.bfloat16)
        grad_query = jnp.einsum(
            "jhqk,jkhd->jqhd", grad_scores, key_tiles, preferred_element_type=jnp.float32
        ).astype(jnp.bfloat16)
        key_part = jnp.einsum(
            "jhqk,jqhd->jkhd", grad_scores, query_set, preferred_element_type=jnp.float32
        ).reshape(4, window_rows, width_hd)
        value_part = jnp.einsum(
            "jhqk,jqhd->jkhd", weights, grad_set, preferred_element_type=jnp.float32
        ).reshape(4, window_rows, width_hd)
        contributions = jnp.stack([key_part, value_part], axis=1)
        for member in range(4):
            offset = starts[member]
            current = lax.dynamic_slice_in_dim(running, offset, window_rows, 1)
            running = lax.dynamic_update_slice_in_dim(
                running, current + contributions[member], offset, 1
            )
        return (
            running,
            (attended.reshape(4 * BLOCK, width_hd), grad_query.reshape(4 * BLOCK, width_hd)),
        )

    empty_sum = jnp.zeros((2, kv_source.shape[1], width_hd), jnp.float32)
    grad_sums, outputs = lax.scan(advance, empty_sum, jnp.arange(set_count, dtype=jnp.int32))
    return (
        grad_sums,
        outputs[0].reshape(rows_dev, width_hd),
        outputs[1].reshape(rows_dev, width_hd),
    )


def body(queries, memory_keys, memory_values, out_weight, grad_out, key_first, key_last):
    query_rows = queries[0]
    dy_rows = grad_out[0]
    first_blocks = key_first[0]
    last_blocks = key_last[0]
    rows_dev, width_hd = query_rows.shape
    block_count = rows_dev // BLOCK
    window_rows = BLOCK + 2 * REACH
    whole_weight = lax.all_gather(out_weight, "seq", axis=0, tiled=True)
    grad_attn = lax.dot_general(
        dy_rows, whole_weight, (((1,), (1,)), ((), ())), preferred_element_type=jnp.float32
    ).astype(jnp.bfloat16)
    stacked = jnp.stack([memory_keys[0], memory_values[0]])
    padded = padded_2(stacked, (("seq", 1),), REACH)
    halo_anchor = lax.axis_index("seq") * rows_dev - REACH
    window_starts = jnp.arange(block_count, dtype=jnp.int32) * BLOCK
    grad_sums, attended, grad_query = run_tiles(
        query_rows,
        grad_attn,
        padded,
        window_starts,
        window_rows,
        first_blocks,
        last_blocks,
        halo_anchor,
    )
    left_rim = grad_sums[:, :REACH]
    right_rim = grad_sums[:, REACH + rows_dev :]
    from_right = passed_along(left_rim.astype(jnp.bfloat16), "seq", -1).astype(left_rim.dtype)
    from_left = passed_along(right_rim.astype(jnp.bfloat16), "seq", 1).astype(right_rim.dtype)
    own_sums = grad_sums[:, REACH : REACH + rows_dev]
    own_sums = own_sums.at[:, :REACH].add(from_left)
    own_sums = own_sums.at[:, rows_dev - REACH :].add(from_right)
    key_grad = own_sums[0].astype(jnp.bfloat16)
    value_grad = own_sums[1].astype(jnp.bfloat16)
    layer_out = jnp.dot(attended, whole_weight, preferred_element_type=jnp.float32).astype(
        jnp.bfloat16
    )
    normalizer = math.sqrt(lax.axis_size("seq") * rows_dev)
    shard_sum = lax.psum_scatter(
        lax.dot_general(
            attended, dy_rows, (((0,), (0,)), ((), ())), preferred_element_type=jnp.float32
        ),
        "seq",
        scatter_dimension=0,
        tiled=True,
    )
    summed = lax.psum(shard_sum.astype(jnp.bfloat16), "dp").astype(jnp.float32)
    weight_grad = summed / normalizer
    return (layer_out[None], grad_query[None], key_grad[None], value_grad[None], weight_grad)


def solution(mesh):
    return jax.shard_map(
        body,
        mesh=mesh,
        in_specs=(
            P("dp", "seq", None),
            P("dp", "seq", None),
            P("dp", "seq", None),
            P("seq", None),
            P("dp", "seq", None),
            P("dp", "seq"),
            P("dp", "seq"),
        ),
        out_specs=(
            P("dp", "seq", None),
            P("dp", "seq", None),
            P("dp", "seq", None),
            P("dp", "seq", None),
            P("seq", None),
        ),
        check_vma=False,
    )
```

profile of v0, /device:TPU:1, one launch (start us, length us, event | category | flops | bytes accessed | tf_op | source)
XLA Modules:
  0.0 403.9 jit_solution(8110936625988158264)
XLA Ops:
  7.2 0.7 all-gather.2.cloned.1.call-update
  8.0 1.3 constant_dynamic-update-slice_fusion.1
  9.3 1.3 constant_dynamic-update-slice_fusion
  10.6 1.3 copy-done.5
  11.9 1.5 fusion.76
  13.4 5.1 %collective-permute-start.1 = (bf16[2,256,1024]{2,1,0:T(8,128)(2,1)}, bf16[2,256,1024]{2,1,0:T(8,128)(2,1)}, u32[]{:S(2)}, u32[]{:S(2)}) collective-permute-start(bf16[2,256,1024]{2,1,0:T(8,128)(2,1)} %get-tuple-element.91), channel_id=1, source_target_pairs={{4,0},{8,4},{12,8},{16,12},{20,16},{24,20},{28,24},{32,28},{36,32}... | collective-permute-start | bytes 3145736 | tf_op jit(solution)/shard_map/ppermute | solution.py:22
  18.5 1.9 collective-permute-start
  20.5 0.6 gather_fusion
  21.3 0.6 gather_fusion.2
  21.9 0.6 gather_fusion.1
  22.6 1.5 copy.54
  24.1 1.5 copy.42
  25.6 5.8 %collective-permute-done.1 = bf16[2,256,1024]{2,1,0:T(8,128)(2,1)} collective-permute-done((bf16[2,256,1024]{2,1,0:T(8,128)(2,1)}, bf16[2,256,1024]{2,1,0:T(8,128)(2,1)}, u32[]{:S(2)}, u32[]{:S(2)}) %collective-permute-start.1) | collective-permute-done | bytes 1048608 | tf_op jit(solution)/shard_map/ppermute | solution.py:22
  31.4 1.5 collective-permute-done
  32.9 3.8 pad_maximum_fusion.1
  36.7 21.0 %while.3 = (s32[]{:T(128)}, bf16[2,1024,1024]{2,1,0:T(8,128)(2,1)}, s32[4,3]{1,0:T(4,128)S(1)}, bf16[4,2,640,1024]{3,2,1,0:T(8,128)(2,1)}, s32[]{:T(128)}) while((s32[]{:T(128)}, bf16[2,1024,1024]{2,1,0:T(8,128)(2,1)}, s32[4,3]{1,0:T(4,128)S(1)}, bf16[4,2,640,1024]{3,2,1,0:T(8,128)(2,1)}, s32[]{:T(128)}) %tuple.39), condition=%wide.while_cond.2, body=%wide.while_body.2.sunk | while | flops 2 | bytes 5243501 | solution.py:46
  37.2 4.6 %bitcast_dynamic-update-slice_fusion.2 = bf16[4,2,640,1024]{3,2,1,0:T(8,128)(2,1)} fusion(bf16[4,2,640,1024]{3,2,1,0:T(8,128)(2,1)} %get-tuple-element.131, s32[]{:T(128)S(6)} %copy.69, bf16[2,1024,1024]{2,1,0:T(8,128)(2,1)} %get-tuple-element.134, s32[]{:T(128)} %bitcast.105), kind=kLoop, calls=%fused_computation.3.clone.1 | loop fusion | bytes 5243396 | tf_op jit(solution)/shard_map/while/body/eval_jaxpr/vmap()/gather
  41.9 0.6 slice.215
  42.5 4.6 %bitcast_dynamic-update-slice_fusion.2 = bf16[4,2,640,1024]{3,2,1,0:T(8,128)(2,1)} fusion(bf16[4,2,640,1024]{3,2,1,0:T(8,128)(2,1)} %get-tuple-element.131, s32[]{:T(128)S(6)} %copy.69, bf16[2,1024,1024]{2,1,0:T(8,128)(2,1)} %get-tuple-element.134, s32[]{:T(128)} %bitcast.105), kind=kLoop, calls=%fused_computation.3.clone.1 | loop fusion | bytes 5243396 | tf_op jit(solution)/shard_map/while/body/eval_jaxpr/vmap()/gather
  47.1 0.6 slice.215
  47.7 4.6 %bitcast_dynamic-update-slice_fusion.2 = bf16[4,2,640,1024]{3,2,1,0:T(8,128)(2,1)} fusion(bf16[4,2,640,1024]{3,2,1,0:T(8,128)(2,1)} %get-tuple-element.131, s32[]{:T(128)S(6)} %copy.69, bf16[2,1024,1024]{2,1,0:T(8,128)(2,1)} %get-tuple-element.134, s32[]{:T(128)} %bitcast.105), kind=kLoop, calls=%fused_computation.3.clone.1 | loop fusion | bytes 5243396 | tf_op jit(solution)/shard_map/while/body/eval_jaxpr/vmap()/gather
  52.3 0.6 slice.215
  52.9 4.7 %bitcast_dynamic-update-slice_fusion.2 = bf16[4,2,640,1024]{3,2,1,0:T(8,128)(2,1)} fusion(bf16[4,2,640,1024]{3,2,1,0:T(8,128)(2,1)} %get-tuple-element.131, s32[]{:T(128)S(6)} %copy.69, bf16[2,1024,1024]{2,1,0:T(8,128)(2,1)} %get-tuple-element.134, s32[]{:T(128)} %bitcast.105), kind=kLoop, calls=%fused_computation.3.clone.1 | loop fusion | bytes 5243396 | tf_op jit(solution)/shard_map/while/body/eval_jaxpr/vmap()/gather
  57.6 5.4 %slice.116 = bf16[4,1,640,1024]{3,2,1,0:T(8,128)(2,1)} slice(bf16[4,2,640,1024]{3,2,1,0:T(8,128)(2,1)} %get-tuple-element.69), slice={[0:4], [1:2], [0:640], [0:1024]} | slice | bytes 10485760 | tf_op jit(solution)/shard_map/while/body/eval_jaxpr/slice | solution.py:49
  63.1 15.3 %copy.30 = bf16[4,2,640,1024]{2,3,0,1:T(8,128)(2,1)} copy(bf16[4,2,640,1024]{3,2,1,0:T(8,128)(2,1)} %get-tuple-element.69) | data formatting | bytes 20971520 | tf_op jit(solution)/shard_map/while/body/eval_jaxpr/vmap()/gather | solution.py:46
  78.3 8.0 %copy.29 = bf16[4,1,640,1024]{2,3,0,1:T(8,128)(2,1)} copy(bf16[4,1,640,1024]{3,2,1,0:T(8,128)(2,1)} %slice.116) | data formatting | bytes 10485760 | tf_op jit(solution)/shard_map/while/body/eval_jaxpr/slice | solution.py:49
  86.3 5.3 %slice.156 = bf16[4,1,640,1024]{2,3,0,1:T(8,128)(2,1)} slice(bf16[4,2,640,1024]{2,3,0,1:T(8,128)(2,1)} %copy.30), slice={[0:4], [0:1], [0:640], [0:1024]} | slice | bytes 10485760 | tf_op jit(solution)/shard_map/while/body/eval_jaxpr/slice | solution.py:48
  91.7 14.1 %bitcast_reduce_fusion = (f32[4,8,128]{2,1,0:T(8,128)S(1)}, f32[4,8,640,128]{3,2,1,0:T(8,128)}) fusion(pred[4,640]{1,0:T(4,128)(4,1)S(1)} %compare_and_fusion, bf16[4,640,8,128]{1,3,2,0:T(8,128)(2,1)} %bitcast.112, bf16[4,128,8,128]{1,3,2,0:T(8,128)(2,1)S(1)} %copy-done.6), kind=kOutput, calls=%fused_computation.14 | convolution fusion | flops 1357906560 | bytes 16796160 | tf_op jit(solution)/shard_map/while/body/eval_jaxpr/sub | solution.py:62
  105.8 8.1 %fusion.50 = bf16[4,128,8,128]{1,3,2,0:T(8,128)(2,1)} fusion(bf16[4,640,8,128]{1,3,2,0:T(8,128)(2,1)} %bitcast.108, f32[4,8,640,128]{3,2,1,0:T(8,128)} %get-tuple-element.97, f32[4,8,128]{2,1,0:T(8,128)S(1)} %get-tuple-element.96), kind=kOutput, calls=%fused_computation.58 | convolution fusion | flops 676855808 | bytes 16793600 | tf_op jit(solution)/shard_map/while/body/eval_jaxpr/jhqk,jkhd->jqhd/dot_general | solution.py:65
  113.9 2.4 copy.34
  116.3 7.0 %fusion.37 = f32[1024,2048]{1,0:T(8,128)} fusion(bf16[1,512,2048]{2,1,0:T(8,128)(2,1)S(1)} %copy-done, bf16[64,8,8,128]{3,2,1,0:T(8,128)(2,1)} %bitcast.117), kind=kOutput, calls=%fused_computation.51 | convolution fusion | flops 2147483648 | bytes 11534336 | tf_op jit(solution)/shard_map/dot_general | solution.py:143
  123.5 0.6 fusion.77
  131.9 4.5 %fusion.56 = bf16[64,8,8,128]{3,1,2,0:T(8,128)(2,1)S(1)} fusion(bf16[1024,2048]{1,0:T(8,128)(2,1)} %all-gather.2.cloned.1.call-done, bf16[1,512,2048]{2,1,0:T(8,128)(2,1)S(1)} %copy-done), kind=kOutput, calls=%fused_computation.60 | convolution fusion | flops 2148007936 | bytes 7340032 | tf_op jit(solution)/shard_map/dot_general | solution.py:112
  136.7 0.8 copy.43
  137.5 7.9 %fusion.78 = f32[4,8,128,640]{2,3,1,0:T(8,128)} fusion(bf16[4,128,8,128]{1,3,2,0:T(8,128)(2,1)S(1)} %copy.43, bf16[4,640,8,128]{1,3,2,0:T(8,128)(2,1)} %bitcast.109), kind=kOutput, calls=%fused_computation.94 | convolution fusion | flops 671088640 | bytes 16777216 | tf_op jit(solution)/shard_map/while/body/eval_jaxpr/jqhd,jkhd->jhqk/dot_general | solution.py:68
  145.4 18.9 %fusion.10 = f32[4,8,640,128]{2,3,1,0:T(8,128)} fusion(bf16[4,128,8,128]{1,3,2,0:T(8,128)(2,1)S(1)} %copy-done.6, f32[4,8,128,640]{2,3,1,0:T(8,128)} %fusion.78, f32[4,8,640,128]{3,2,1,0:T(8,128)} %get-tuple-element.97, f32[4,8,128]{2,1,0:T(8,128)S(1)} %get-tuple-element.96), kind=kOutput, calls=%fused_computation.22 | convolution fusion | flops 689443456 | bytes 32522240 | tf_op jit(solution)/shard_map/while/body/eval_jaxpr/jhqk,jqhd->jkhd/dot_general | solution.py:76
  164.3 11.5 %copy.45 = f32[4,1,640,1024]{3,2,1,0:T(8,128)} copy(f32[4,1,640,1024]{2,3,0,1:T(8,128)} %bitcast.110) | data formatting | bytes 20971520 | tf_op jit(solution)/shard_map/while/body/eval_jaxpr/stack;while/body/eval_jaxpr/reshape | solution.py:82
  175.7 10.2 %fusion.31 = f32[4,8,128,640]{3,2,1,0:T(8,128)} fusion(bf16[4,128,8,128]{1,3,2,0:T(8,128)(2,1)S(1)} %copy.43, f32[4,8,640,128]{3,2,1,0:T(8,128)} %get-tuple-element.97, f32[4,8,128]{2,1,0:T(8,128)S(1)} %get-tuple-element.96), kind=kOutput, calls=%fused_computation.43 | convolution fusion | flops 676331520 | bytes 22036480 | tf_op jit(solution)/shard_map/while/body/eval_jaxpr/jhqk,jqhd->jkhd/dot_general | solution.py:79
  185.9 11.4 %copy.46 = f32[4,1,640,1024]{3,2,1,0:T(8,128)} copy(f32[4,1,640,1024]{2,3,0,1:T(8,128)} %bitcast.111) | data formatting | bytes 20971520 | tf_op jit(solution)/shard_map/while/body/eval_jaxpr/stack;while/body/eval_jaxpr/reshape | solution.py:82
  197.4 5.7 %fusion.19 = f32[2,640,1024]{2,1,0:T(8,128)} fusion(f32[4,1,640,1024]{3,2,1,0:T(8,128)} %copy.45, f32[4,1,640,1024]{3,2,1,0:T(8,128)} %copy.46), kind=kLoop, calls=%fused_computation.28 | loop fusion | flops 1310720 | bytes 26214400 | tf_op jit(solution)/shard_map/while/body/eval_jaxpr/squeeze | solution.py:87
  203.0 4.3 %broadcast_in_dim.65 = f32[2,1024,1024]{2,1,0:T(8,128)} broadcast(f32[]{:T(128)} %constant.118.clone.1), dimensions={} | broadcast | bytes 8388612 | tf_op jit(solution)/shard_map/broadcast_in_dim | solution.py:94
  207.3 15.0 %dynamic_update_slice.21 = f32[2,1024,1024]{2,1,0:T(8,128)} dynamic-update-slice(f32[2,1024,1024]{2,1,0:T(8,128)} %broadcast_in_dim.65, f32[2,640,1024]{2,1,0:T(8,128)} %fusion.19, s32[]{:T(128)} %constant.105.clone.1, s32[]{:T(128)S(6)} %select_n.64, s32[]{:T(128)} %constant.105.clone.1) | dynamic-update-slice | bytes 10485764 | tf_op jit(solution)/shard_map/while/body/eval_jaxpr/dynamic_update_slice | solution.py:86
  222.4 8.5 %fusion.22 = f32[2,640,1024]{2,1,0:T(8,128)} fusion(f32[4,1,640,1024]{3,2,1,0:T(8,128)} %copy.45, f32[4,1,640,1024]{3,2,1,0:T(8,128)} %copy.46, f32[2,1024,1024]{2,1,0:T(8,128)} %dynamic_update_slice.21, s32[]{:T(128)S(6)} %select_n.65), kind=kLoop, calls=%fused_computation.31 | loop fusion | flops 2621440 | bytes 31457284 | tf_op jit(solution)/shard_map/while/body/eval_jaxpr/add | solution.py:87
  230.9 14.9 %dynamic_update_slice.22 = f32[2,1024,1024]{2,1,0:T(8,128)} dynamic-update-slice(f32[2,1024,1024]{2,1,0:T(8,128)} %dynamic_update_slice.21, f32[2,640,1024]{2,1,0:T(8,128)} %fusion.22, s32[]{:T(128)} %constant.105.clone.1, s32[]{:T(128)S(6)} %select_n.65, s32[]{:T(128)} %constant.105.clone.1) | dynamic-update-slice | bytes 10485764 | tf_op jit(solution)/shard_map/while/body/eval_jaxpr/dynamic_update_slice | solution.py:86
  245.8 8.3 %fusion.17 = f32[2,640,1024]{2,1,0:T(8,128)} fusion(f32[4,1,640,1024]{3,2,1,0:T(8,128)} %copy.45, f32[4,1,640,1024]{3,2,1,0:T(8,128)} %copy.46, f32[2,1024,1024]{2,1,0:T(8,128)} %dynamic_update_slice.22, s32[]{:T(128)S(6)} %select_n.66), kind=kLoop, calls=%fused_computation.26 | loop fusion | flops 2621440 | bytes 31457284 | tf_op jit(solution)/shard_map/while/body/eval_jaxpr/add | solution.py:87
  254.1 14.9 %dynamic_update_slice.23 = f32[2,1024,1024]{2,1,0:T(8,128)} dynamic-update-slice(f32[2,1024,1024]{2,1,0:T(8,128)} %dynamic_update_slice.22, f32[2,640,1024]{2,1,0:T(8,128)} %fusion.17, s32[]{:T(128)} %constant.105.clone.1, s32[]{:T(128)S(6)} %select_n.66, s32[]{:T(128)} %constant.105.clone.1) | dynamic-update-slice | bytes 10485764 | tf_op jit(solution)/shard_map/while/body/eval_jaxpr/dynamic_update_slice | solution.py:86
  268.9 8.3 %fusion.24 = f32[2,640,1024]{2,1,0:T(8,128)} fusion(f32[4,1,640,1024]{3,2,1,0:T(8,128)} %copy.46, f32[4,1,640,1024]{3,2,1,0:T(8,128)} %copy.45, f32[2,1024,1024]{2,1,0:T(8,128)} %dynamic_update_slice.23, s32[]{:T(128)S(6)} %select_n.67), kind=kLoop, calls=%fused_computation.34 | loop fusion | flops 2621440 | bytes 31457284 | tf_op jit(solution)/shard_map/while/body/eval_jaxpr/add | solution.py:87
  277.2 14.3 %dynamic_update_slice.24 = f32[2,1024,1024]{2,1,0:T(8,128)} dynamic-update-slice(f32[2,1024,1024]{2,1,0:T(8,128)} %dynamic_update_slice.23, f32[2,640,1024]{2,1,0:T(8,128)} %fusion.24, s32[]{:T(128)} %constant.105.clone.1, s32[]{:T(128)S(6)} %select_n.67, s32[]{:T(128)} %constant.105.clone.1) | dynamic-update-slice | bytes 10485764 | tf_op jit(solution)/shard_map/while/body/eval_jaxpr/dynamic_update_slice | solution.py:86
  291.5 4.0 convert.8
  295.5 1.5 fusion.74
  297.1 4.4 %collective-permute-start.2 = (bf16[2,256,1024]{2,1,0:T(8,128)(2,1)}, bf16[2,256,1024]{2,1,0:T(8,128)(2,1)}, u32[]{:S(2)}, u32[]{:S(2)}) collective-permute-start(bf16[2,256,1024]{2,1,0:T(8,128)(2,1)} %get-tuple-element.87), channel_id=1, source_target_pairs={{0,4},{4,8},{8,12},{12,16},{16,20},{20,24},{24,28},{28,32},{32,36}... | collective-permute-start | bytes 3145736 | tf_op jit(solution)/shard_map/ppermute | solution.py:30
  301.5 1.9 collective-permute-start.3
  303.4 19.4 %fusion.53 = bf16[4,128,8,128]{1,3,2,0:T(8,128)(2,1)} fusion(bf16[4,640,8,128]{1,3,2,0:T(8,128)(2,1)} %bitcast.113, f32[4,8,128,640]{2,3,1,0:T(8,128)} %fusion.78, f32[4,8,640,128]{3,2,1,0:T(8,128)} %get-tuple-element.97, f32[4,8,128]{2,1,0:T(8,128)S(1)} %get-tuple-element.96), kind=kOutput, calls=%fused_computation.59 | convolution fusion | flops 689967744 | bytes 27279360 | tf_op jit(solution)/shard_map/while/body/eval_jaxpr/jhqk,jkhd->jqhd/dot_general | solution.py:73
  322.9 5.0 %slice.163 = f32[2,512,1024]{2,1,0:T(8,128)} slice(f32[2,1024,1024]{2,1,0:T(8,128)} %dynamic_update_slice.24), slice={[0:2], [256:768], [0:1024]} | slice | bytes 8388608 | tf_op jit(solution)/shard_map/slice | solution.py:133
  327.8 1.7 copy.40
  329.5 1.3 broadcast_in_dim.64
  330.8 6.0 %fusion.30 = bf16[1,512,2048]{2,1,0:T(8,128)(2,1)} fusion(bf16[1024,2048]{1,0:T(8,128)(2,1)} %all-gather.2.cloned.1.call-done, bf16[64,8,8,128]{3,2,1,0:T(8,128)(2,1)S(1)} %bitcast.118), kind=kOutput, calls=%fused_computation.42 | convolution fusion | flops 2148532224 | bytes 7340032 | tf_op jit(solution)/shard_map/dot_general | solution.py:138
  336.8 2.3 fusion.36
  339.1 0.6 fusion.35
  339.7 1.7 convert.9
  341.4 1.5 convert_element_type.56
  342.9 3.0 fusion.75
  346.0 49.9 %all-reduce.2.cloned.1.call-done = bf16[16,2048]{1,0:T(8,128)(2,1)} async-done(((bf16[16,2048]{1,0:T(8,128)(2,1)}), bf16[16,2048]{1,0:T(8,128)(2,1)}) %all-reduce.2.cloned.1.call-update) | async-done | bytes 65552 | tf_op jit(solution)/shard_map/psum | solution.py:150
  395.8 1.5 convert_multiply_fusion
  (40 shorter events, 1.5 us)
Async XLA Ops:
  7.2 109.1 %copy-start = (bf16[1,512,2048]{2,1,0:T(8,128)(2,1)S(1)}, bf16[1,512,2048]{2,1,0:T(8,128)(2,1)}, u32[]{:S(2)}) copy-start(bf16[1,512,2048]{2,1,0:T(8,128)(2,1)} %param.15) | copy-start | bytes 6291460
  7.2 14.1 %copy-start.2 = (s32[1,4]{1,0:T(1,128)S(1)}, s32[1,4]{1,0:T(1,128)}, u32[]{:S(2)}) copy-start(s32[1,4]{1,0:T(1,128)} %param.17) | copy-start | bytes 52
  7.2 14.7 %copy-start.3 = (s32[1,4]{1,0:T(1,128)S(1)}, s32[1,4]{1,0:T(1,128)}, u32[]{:S(2)}) copy-start(s32[1,4]{1,0:T(1,128)} %param.16) | copy-start | bytes 52
  7.2 124.6 %all-gather.2.cloned.1.call-start = ((), (), s32[]{:S(2)}) async-start(), calls=%async_computation.1 | async-start | bytes 4259840 | tf_op jit(solution)/shard_map/all_gather | solution.py:111
  7.9 333.4 %reduce-scatter.2.cloned.1.call-start = ((), (), s32[]{:S(2)}) async-start(), calls=%async_computation.2 | async-start | bytes 8519680 | tf_op jit(solution)/shard_map/reduce_scatter | solution.py:142
  10.6 1.3 copy-start.5
  13.4 18.0 %collective-permute-start.1 = (bf16[2,256,1024]{2,1,0:T(8,128)(2,1)}, bf16[2,256,1024]{2,1,0:T(8,128)(2,1)}, u32[]{:S(2)}, u32[]{:S(2)}) collective-permute-start(bf16[2,256,1024]{2,1,0:T(8,128)(2,1)} %get-tuple-element.91), channel_id=1, source_target_pairs={{4,0},{8,4},{12,8},{16,12},{20,16},{24,20},{28,24},{32,28},{36,32}... | collective-permute-start | bytes 3145736 | tf_op jit(solution)/shard_map/ppermute | solution.py:22
  18.5 14.4 %collective-permute-start = (bf16[2,256,1024]{2,1,0:T(8,128)(2,1)}, bf16[2,256,1024]{2,1,0:T(8,128)(2,1)}, u32[]{:S(2)}, u32[]{:S(2)}) collective-permute-start(bf16[2,256,1024]{2,1,0:T(8,128)(2,1)} %get-tuple-element.90), channel_id=1, source_target_pairs={{0,4},{4,8},{8,12},{12,16},{16,20},{20,24},{24,28},{28,32},{32,36}... | collective-permute-start | bytes 3145736 | tf_op jit(solution)/shard_map/ppermute | solution.py:19
  78.3 13.4 %copy-start.6 = (bf16[4,128,8,128]{1,3,2,0:T(8,128)(2,1)S(1)}, bf16[4,128,8,128]{1,3,2,0:T(8,128)(2,1)}, u32[]{:S(2)}) copy-start(bf16[4,128,8,128]{1,3,2,0:T(8,128)(2,1)} %copy.42) | copy-start | bytes 3145732
  123.2 272.6 %all-reduce.2.cloned.1.call-start = ((), (), s32[]{:S(2)}) async-start(), calls=%async_computation.3 | async-start | bytes 131072 | tf_op jit(solution)/shard_map/psum | solution.py:150
  297.1 39.7 %collective-permute-start.2 = (bf16[2,256,1024]{2,1,0:T(8,128)(2,1)}, bf16[2,256,1024]{2,1,0:T(8,128)(2,1)}, u32[]{:S(2)}, u32[]{:S(2)}) collective-permute-start(bf16[2,256,1024]{2,1,0:T(8,128)(2,1)} %get-tuple-element.87), channel_id=1, source_target_pairs={{0,4},{4,8},{8,12},{12,16},{16,20},{20,24},{24,28},{28,32},{32,36}... | collective-permute-start | bytes 3145736 | tf_op jit(solution)/shard_map/ppermute | solution.py:30
  301.5 37.6 %collective-permute-start.3 = (bf16[2,256,1024]{2,1,0:T(8,128)(2,1)}, bf16[2,256,1024]{2,1,0:T(8,128)(2,1)S(1)}, u32[]{:S(2)}, u32[]{:S(2)}) collective-permute-start(bf16[2,256,1024]{2,1,0:T(8,128)(2,1)} %get-tuple-element.86), channel_id=1, source_target_pairs={{4,0},{8,4},{12,8},{16,12},{20,16},{24,20},{28,24},{32,28},{36,32}... | collective-permute-start | bytes 3145736 | tf_op jit(solution)/shard_map/ppermute | solution.py:30
  322.9 7.9 %copy-start.7 = (bf16[4,128,8,128]{3,2,1,0:T(8,128)(2,1)S(1)}, bf16[4,128,8,128]{3,2,1,0:T(8,128)(2,1)}, u32[]{:S(2)}) copy-start(bf16[4,128,8,128]{3,2,1,0:T(8,128)(2,1)} %copy.34) | copy-start | bytes 3145732
  330.8 6.0 %copy-start.4 = (f32[2,512,1024]{2,1,0:T(8,128)S(1)}, f32[2,512,1024]{2,1,0:T(8,128)}, u32[]{:S(2)}) copy-start(f32[2,512,1024]{2,1,0:T(8,128)} %slice.163) | copy-start | bytes 12582916
  336.8 60.6 %copy-start.1 = (bf16[1,512,2048]{2,1,0:T(8,128)(2,1)S(1)}, bf16[1,512,2048]{2,1,0:T(8,128)(2,1)}, u32[]{:S(2)}) copy-start(bf16[1,512,2048]{2,1,0:T(8,128)(2,1)} %param.15) | copy-start | bytes 6291460
Sparse Core Ops, SparseCore 0:
  10.8 83.3 all-gather.1
  123.4 153.1 reduce-scatter.1
  343.1 52.7 all-reduce.1
where the time goes:
time: 408 us; the launch traced here: 404 us
  local copies, waits for them, and re-layouts  168 us (41%)
  matrix products  96.1 us (24%)
  waiting for transfers between devices  57.9 us (14%)
  other arithmetic  46.3 us (11%)
  between operations  21.7 us (5%)
  starting transfers between devices  13.7 us (3%)
    dynamic_update_slice x4, local copies, waits for them, and re-layouts, advance(): lax.dynamic_update_slice_in_dim(running, current + contributions[member],...  59.1 us
    psum x1, waiting for transfers between devices, body(): summed = lax.psum(shard_sum.astype(jnp.bfloat16), 'dp').astype(jnp.float32)  49.9 us
    add x3, other arithmetic, advance(): current + contributions[member]  25.1 us
    reshape x2, local copies, waits for them, and re-layouts, advance(): contributions = jnp.stack([key_part, value_part], axis=1)  22.9 us
    gather x12, local copies, waits for them, and re-layouts  20.9 us
    dot_general x1, matrix products, advance(): jnp.einsum('jhqk,jkhd->jqhd', grad_scores, key_tiles, preferred_element_t...  19.4 us
    dot_general x1, matrix products, advance(): jnp.einsum('jhqk,jqhd->jkhd', grad_scores, query_set, preferred_element_t...  18.9 us
    gather x1, local copies, waits for them, and re-layouts, advance(): lax.dynamic_slice_in_dim(kv_source, offset, window_rows, 1)  15.3 us
  transfers between devices with their start and end apart: 7, of which 3 were waited for; matrix products, arithmetic and copies ran while one was open for 76% of the time, Pallas kernels for 0%

commit v1 on v0

v1 whole, which is shorter than its diff:
```python
import functools
import math

import jax
import jax.numpy as jnp
from jax import lax
from jax.experimental import pallas as pl
from jax.experimental.pallas import tpu as pltpu
from jax.sharding import PartitionSpec as P

HDIM = 128
BLOCK = 128
HALF = 256
CORES = 2
Y_CHIPS = 4
F32 = jnp.float32
BF16 = jnp.bfloat16
NEVER = -1e30


def dot(a, b, dims):
    return lax.dot_general(a, b, (dims, ((), ())), preferred_element_type=F32)


def kernel(
    sizes,
    q_hbm, k_hbm, v_hbm, shard_hbm, go_hbm, first_ref, last_ref,
    layer_hbm, dq_hbm, dk_hbm, dv_hbm, wgrad_hbm,
    w, q, kg, vg, go, probs, attn_t, attn, ga, bias,
    dq, dk_own, dv_own, dk_send, dv_send, dk_recv, dv_recv, layer,
    wg, sib_recv, plus_send, plus_recv, minus_send, minus_recv,
    z_sum, y_send, y_recv, x_all, wgrad,
    load_sem, store_sem,
    halo_send_sem, halo_recv_sem,
    agy_send_sem, agy_recv_sem, agp_send_sem, agp_recv_sem, agm_send_sem, agm_recv_sem,
    ags_send_sem, ags_recv_sem,
    rss_send_sem, rss_recv_sem, rsp_send_sem, rsp_recv_sem, rsm_send_sem, rsm_recv_sem,
    rsy_send_sem, rsy_recv_sem, rsx_send_sem, rsx_recv_sem,
    grad_send_sem, grad_recv_sem,
):
    n_seq, n_x, n_y, n_z, n_plus, n_minus, heads, width, norm = sizes
    scale = 1.0 / math.sqrt(HDIM)
    s = lax.axis_index("seq")
    x = lax.axis_index("dp")
    c = s % CORES
    zy = s // CORES
    y = zy % n_y
    z = zy // n_y

    def at_zy(z_index, y_index, core):
        return (z_index * n_y + y_index) * CORES + core

    sibling = s + 1 - 2 * c
    across = (s + 2 * c - 1 + n_seq) % n_seq
    z_next = at_zy((z + 1) % n_z, y, c)
    z_prev = at_zy((z + n_z - 1) % n_z, y, c)
    y_peers = [at_zy(z, (y + j) % n_y, c) for j in range(1, n_y)]
    x_peers = [(x + j) % n_x for j in range(1, n_x)]
    partners = (sibling, across)
    group = (1 - c, c)

    loads = []

    def load(src, dst):
        copy = pltpu.make_async_copy(src, dst, load_sem.at[len(loads)])
        copy.start()
        loads.append(copy)
        return copy

    def token_rows(t):
        return pl.ds(pl.multiple_of(group[t] * HALF, HALF), HALF)

    load_shard = load(shard_hbm, w.at[zy, c])
    load_q, load_k, load_v, load_go = [], [], [], []
    for t in range(2):
        load_q.append(load(q_hbm.at[token_rows(t)], q.at[t]))
        load_k.append(load(k_hbm.at[token_rows(t)], kg.at[t, pl.ds(0, HALF)]))
        load_v.append(load(v_hbm.at[token_rows(t)], vg.at[t, pl.ds(0, HALF)]))
    for t in range(2):
        load_go.append(load(go_hbm.at[token_rows(t)], go.at[t]))

    barrier = pltpu.get_barrier_semaphore()
    seq_peers = [sibling, across, z_next, z_prev] + y_peers
    for peer in seq_peers:
        pl.semaphore_signal(
            barrier, inc=1, device_id={"seq": peer}, device_id_type=pl.DeviceIdType.MESH
        )
    for peer in x_peers:
        pl.semaphore_signal(
            barrier, inc=1, device_id={"dp": peer}, device_id_type=pl.DeviceIdType.MESH
        )
    pl.semaphore_wait(barrier, len(seq_peers) + len(x_peers))

    sent = []

    def send(src, dst, send_sem, recv_sem, target):
        copy = pltpu.make_async_remote_copy(
            src_ref=src,
            dst_ref=dst,
            send_sem=send_sem,
            recv_sem=recv_sem,
            device_id=target,
            device_id_type=pl.DeviceIdType.MESH,
        )
        copy.start()
        sent.append(copy)
        return copy

    agy = [
        send(
            shard_hbm, w.at[zy, c], agy_send_sem.at[j], agy_recv_sem.at[j], {"seq": peer}
        )
        for j, peer in enumerate(y_peers)
    ]

    halo = []
    for t in (1, 0):
        for which, (src, dst) in enumerate(((k_hbm, kg), (v_hbm, vg))):
            halo.append(
                send(
                    src.at[token_rows(t)],
                    dst.at[t, pl.ds(HALF, HALF)],
                    halo_send_sem.at[t * 2 + which],
                    halo_recv_sem.at[t * 2 + which],
                    {"seq": partners[t]},
                )
            )
    halo = {1: halo[:2], 0: halo[2:]}

    def slab(z_index):
        return w.at[pl.ds(z_index * n_y, n_y), c]

    ag_sib = []

    def share_slab(z_index):
        i = len(ag_sib)
        ag_sib.append(
            send(
                slab(z_index), slab(z_index), ags_send_sem.at[i], ags_recv_sem.at[i],
                {"seq": sibling},
            )
        )

    agp, agm = [], []

    def ag_step(k):
        if k == 0:
            load_shard.wait()
            for copy in agy:
                copy.wait_recv()
        from_prev, from_next = (z + n_z - k) % n_z, (z + k) % n_z
        if 0 < k <= n_plus:
            agp[k - 1].wait_recv()
        if k < n_plus:
            agp.append(
                send(
                    slab(from_prev), slab(from_prev), agp_send_sem.at[k], agp_recv_sem.at[k],
                    {"seq": z_next},
                )
            )
        if 0 < k <= n_minus:
            agm[k - 1].wait_recv()
        if k < n_minus:
            agm.append(
                send(
                    slab(from_next), slab(from_next), agm_send_sem.at[k], agm_recv_sem.at[k],
                    {"seq": z_prev},
                )
            )
        if k <= n_plus:
            share_slab(from_prev)
        if 0 < k <= n_minus:
            share_slab(from_next)

    for t in range(2):
        key_row = lax.broadcasted_iota(jnp.int32, (2 * HALF, HALF), 0)
        query_col = lax.broadcasted_iota(jnp.int32, (2 * HALF, HALF), 1)
        own_base = s * 4 + 2 * group[t]
        halo_base = s * 4 - 2 + 6 * group[t]
        key_block = jnp.where(
            key_row < HALF,
            own_base + (key_row >> 7),
            halo_base - 2 + (key_row >> 7),
        )
        early = query_col < BLOCK
        lower = jnp.where(early, first_ref[0, 2 * group[t]], first_ref[0, 2 * group[t] + 1])
        upper = jnp.where(early, last_ref[0, 2 * group[t]], last_ref[0, 2 * group[t] + 1])
        inside = (key_block >= lower) & (key_block < upper)
        bias[t] = jnp.where(inside, 0.0, NEVER)

    def columns(h):
        return pl.ds(pl.multiple_of(h * HDIM, HDIM), HDIM)

    def forward(t):
        load_q[t].wait()
        load_k[t].wait()
        load_v[t].wait()
        for copy in halo[t]:
            copy.wait_recv()

        def head(h, carry):
            cols = columns(h)
            scores = dot(kg[t, :, cols], q[t, :, cols], ((1,), (1,))) * scale + bias[t]
            highest = jnp.max(scores, axis=0, keepdims=True)
            raised = jnp.exp(scores - highest)
            total = jnp.sum(raised, axis=0, keepdims=True)
            p = raised * (1.0 / total)
            probs[t, h] = p
            out_t = dot(vg[t, :, cols], p.astype(BF16), ((0,), (0,)))
            attn_t[pl.ds(pl.multiple_of(h * HDIM, HDIM), HDIM), pl.ds(t * HALF, HALF)] = (
                out_t.astype(BF16)
            )
            attn[pl.ds(t * HALF, HALF), cols] = out_t.T.astype(BF16)
            return carry

        lax.fori_loop(0, heads, head, 0)

    def backward(t):
        def head(h, carry):
            cols = columns(h)
            p = probs[t, h]
            grad_rows = ga[pl.ds(t * HALF, HALF), cols]
            grad_p = dot(vg[t, :, cols], grad_rows, ((1,), (1,)))
            row_term = jnp.sum(p * grad_p, axis=0, keepdims=True)
            grad_s = (p * (grad_p - row_term) * scale).astype(BF16)
            dq_t = dot(kg[t, :, cols], grad_s, ((0,), (0,)))
            dq[t, :, cols] = dq_t.T.astype(BF16)
            dk = dot(grad_s, q[t, :, cols], ((1,), (0,)))
            dv = dot(p.astype(BF16), grad_rows, ((1,), (0,)))
            dk_own[t, :, cols] = dk[:HALF]
            dv_own[t, :, cols] = dv[:HALF]
            dk_send[t, :, cols] = dk[HALF:].astype(BF16)
            dv_send[t, :, cols] = dv[HALF:].astype(BF16)
            return carry

        lax.fori_loop(0, heads, head, 0)
        return [
            send(
                src.at[t], dst.at[t], grad_send_sem.at[2 * t + i], grad_recv_sem.at[2 * t + i],
                {"seq": partners[t]},
            )
            for i, (src, dst) in enumerate(((dk_send, dk_recv), (dv_send, dv_recv)))
        ]

    ag_step(0)
    forward(0)
    ag_step(1)
    forward(1)
    if n_plus >= 2:
        ag_step(2)

    for copy in load_go:
        copy.wait()
    hd = heads * HDIM
    row_blocks, col_width = hd // HALF, min(512, width)

    def weight_tile(i, carry):
        r, n = i % row_blocks, i // row_blocks
        cols = pl.ds(pl.multiple_of(n * col_width, col_width), col_width)
        left = attn_t[pl.ds(pl.multiple_of(r * HALF, HALF), HALF), :]
        right = go[:, :, cols].reshape(2 * HALF, col_width)
        tile = dot(left, right, ((1,), (0,))).astype(BF16)
        wg[pl.ds(r * 8, 8), :, :, cols] = tile.reshape(8, CORES, 16, col_width)
        return carry

    lax.fori_loop(0, row_blocks * (width // col_width), weight_tile, 0)

    order = []
    for k in range(max(n_plus, n_minus), 0, -1):
        if k <= n_plus:
            order.append((1, k))
        if k <= n_minus:
            order.append((-1, k))
    order.append((1, 0))
    rss = {}
    for i, (way, k) in enumerate(order):
        d = (z + way * k + n_z) % n_z
        rss[way, k] = send(
            wg.at[pl.ds(d * n_y, n_y), 1 - c], sib_recv.at[i], rss_send_sem.at[i],
            rss_recv_sem.at[i], {"seq": sibling},
        )
    rsp, rsm = {}, {}

    def chain(way, k):
        i = order.index((way, k))
        d = (z + way * k + n_z) % n_z
        rss[way, k].wait_recv()
        arrivals = []
        if (way == 1 or k == 0) and k < n_plus:
            rsp[k + 1].wait_recv()
            arrivals.append(plus_recv)
        if (way == -1 or k == 0) and k < n_minus:
            rsm[k + 1].wait_recv()
            arrivals.append(minus_recv)

        def add(j, carry):
            total = wg[d * n_y + j, c].astype(F32) + sib_recv[i, j].astype(F32)
            for ref in arrivals:
                total = total + ref[k, j].astype(F32)
            if k == 0:
                z_sum[j] = total
                y_send[j] = total.astype(BF16)
            elif way == 1:
                plus_send[k - 1, j] = total.astype(BF16)
            else:
                minus_send[k - 1, j] = total.astype(BF16)
            return carry

        lax.fori_loop(0, n_y, add, 0)
        if k and way == 1:
            rsp[k] = send(
                plus_send.at[k - 1], plus_recv.at[k - 1], rsp_send_sem.at[k - 1],
                rsp_recv_sem.at[k - 1], {"seq": z_next},
            )
        if k and way == -1:
            rsm[k] = send(
                minus_send.at[k - 1], minus_recv.at[k - 1], rsm_send_sem.at[k - 1],
                rsm_recv_sem.at[k - 1], {"seq": z_prev},
            )

    def chain_level(k):
        if k <= n_plus:
            chain(1, k)
        if 0 < k <= n_minus:
            chain(-1, k)

    chain_level(n_plus)
    for k in range(3, n_plus + 1):
        ag_step(k)
    for copy in ag_sib:
        copy.wait_recv()

    def grad_tile(i, carry):
        rows = w[pl.ds(i * 8, 8)].reshape(HALF, width)
        tile = dot(go[...].reshape(2 * HALF, width), rows, ((1,), (1,)))
        ga[:, pl.ds(pl.multiple_of(i * HALF, HALF), HALF)] = tile.astype(BF16)
        return carry

    lax.fori_loop(0, row_blocks, grad_tile, 0)

    levels = list(range(n_plus - 1, 0, -1))
    grads = {}
    if levels:
        chain_level(levels.pop(0))
    grads[1] = backward(1)
    if levels:
        chain_level(levels.pop(0))
    grads[0] = backward(0)
    for k in levels:
        chain_level(k)
    chain_level(0)

    stores = []

    def store(src, dst):
        copy = pltpu.make_async_copy(src, dst, store_sem.at[len(stores)])
        copy.start()
        stores.append(copy)

    rsy = [
        send(
            y_send.at[(y + j) % n_y], y_recv.at[j - 1], rsy_send_sem.at[j - 1],
            rsy_recv_sem.at[j - 1], {"seq": peer},
        )
        for j, peer in enumerate(y_peers, 1)
    ]
    for t in range(2):
        store(dq.at[t], dq_hbm.at[token_rows(t)])

    tiles = width // HALF

    def layer_tile(i, carry):
        cols = pl.ds(pl.multiple_of(i * HALF, HALF), HALF)
        right = w[:, :, :, cols].reshape(hd, HALF)
        layer[:, cols] = dot(attn[...], right, ((1,), (0,))).astype(BF16)
        return carry

    lax.fori_loop(0, tiles // 2, layer_tile, 0)

    total = z_sum[y]
    for j, copy in enumerate(rsy):
        copy.wait_recv()
        total = total + y_recv[j].astype(F32)
    x_all[x] = total.astype(BF16)
    rsx = [
        send(
            x_all.at[x], x_all.at[x], rsx_send_sem.at[j], rsx_recv_sem.at[j], {"dp": peer}
        )
        for j, peer in enumerate(x_peers)
    ]
    lax.fori_loop(tiles // 2, tiles, layer_tile, 0)
    for t in range(2):
        store(layer.at[pl.ds(t * HALF, HALF)], layer_hbm.at[token_rows(t)])

    for t in (0, 1):
        for copy in grads[t]:
            copy.wait()
        for own, got, out, hbm in (
            (dk_own, dk_recv, dk_send, dk_hbm), (dv_own, dv_recv, dv_send, dv_hbm)
        ):
            def add_rows(i, carry, own=own, got=got, out=out, t=t):
                rows = pl.ds(pl.multiple_of(i * 32, 32), 32)
                out[t, rows] = (own[t, rows] + got[t, rows].astype(F32)).astype(BF16)
                return carry

            lax.fori_loop(0, HALF // 32, add_rows, 0)
            store(out.at[t], hbm.at[token_rows(t)])

    for copy in rsx:
        copy.wait_recv()
    total = x_all[0].astype(F32)
    for j in range(1, n_x):
        total = total + x_all[j].astype(F32)
    wgrad[...] = total * (1.0 / norm)
    store(wgrad, wgrad_hbm)

    waited = grads[0] + grads[1]
    for copy in sent:
        if not any(copy is other for other in waited):
            copy.wait_send()
    for copy in stores:
        copy.wait()


def body(n_seq, n_x, n_y, queries, memory_keys, memory_values, out_weight, grad_out, key_first, key_last):
    rows, hd = queries.shape[1:]
    width = grad_out.shape[2]
    heads = hd // HDIM
    n_z = n_seq // (CORES * n_y)
    n_plus = n_z // 2
    n_minus = n_z - 1 - n_plus
    n_zy = n_z * n_y
    norm = math.sqrt(n_seq * rows)
    sizes = (n_seq, n_x, n_y, n_z, n_plus, n_minus, heads, width, norm)
    vmem, dma = pltpu.VMEM, pltpu.SemaphoreType.DMA
    scratch = [
        vmem((n_zy, CORES, 16, width), BF16),
        vmem((2, HALF, hd), BF16),
        vmem((2, 2 * HALF, hd), BF16),
        vmem((2, 2 * HALF, hd), BF16),
        vmem((2, HALF, width), BF16),
        vmem((2, heads, 2 * HALF, HALF), F32),
        vmem((hd, 2 * HALF), BF16),
        vmem((2 * HALF, hd), BF16),
        vmem((2 * HALF, hd), BF16),
        vmem((2, 2 * HALF, HALF), F32),
        vmem((2, HALF, hd), BF16),
        vmem((2, HALF, hd), F32),
        vmem((2, HALF, hd), F32),
        vmem((2, HALF, hd), BF16),
        vmem((2, HALF, hd), BF16),
        vmem((2, HALF, hd), BF16),
        vmem((2, HALF, hd), BF16),
        vmem((2 * HALF, width), BF16),
        vmem((n_zy, CORES, 16, width), BF16),
        vmem((n_z, n_y, 16, width), BF16),
        vmem((n_plus, n_y, 16, width), BF16),
        vmem((n_plus, n_y, 16, width), BF16),
        vmem((max(n_minus, 1), n_y, 16, width), BF16),
        vmem((max(n_minus, 1), n_y, 16, width), BF16),
        vmem((n_y, 16, width), F32),
        vmem((n_y, 16, width), BF16),
        vmem((n_y - 1, 16, width), BF16),
        vmem((n_x, 16, width), BF16),
        vmem((16, width), F32),
        dma((9,)),
        dma((9,)),
        dma((4,)), dma((4,)),
        dma((n_y - 1,)), dma((n_y - 1,)),
        dma((n_plus,)), dma((n_plus,)),
        dma((max(n_minus, 1),)), dma((max(n_minus, 1),)),
        dma((n_z,)), dma((n_z,)),
        dma((n_z,)), dma((n_z,)),
        dma((n_plus,)), dma((n_plus,)),
        dma((max(n_minus, 1),)), dma((max(n_minus, 1),)),
        dma((n_y - 1,)), dma((n_y - 1,)),
        dma((n_x - 1,)), dma((n_x - 1,)),
        dma((4,)), dma((4,)),
    ]
    hbm = pl.BlockSpec(memory_space=pl.ANY)
    smem = pl.BlockSpec(memory_space=pltpu.SMEM)
    layer_out, grad_query, grad_keys, grad_values, weight_grad = pl.pallas_call(
        functools.partial(kernel, sizes),
        out_shape=(
            jax.ShapeDtypeStruct((rows, width), BF16),
            jax.ShapeDtypeStruct((rows, hd), BF16),
            jax.ShapeDtypeStruct((rows, hd), BF16),
            jax.ShapeDtypeStruct((rows, hd), BF16),
            jax.ShapeDtypeStruct((16, width), F32),
        ),
        in_specs=[hbm] * 5 + [smem] * 2,
        out_specs=(hbm,) * 5,
        scratch_shapes=scratch,
        compiler_params=pltpu.CompilerParams(
            collective_id=0, has_side_effects=True, vmem_limit_bytes=60 * 1024 * 1024
        ),
    )(
        queries[0], memory_keys[0], memory_values[0], out_weight, grad_out[0], key_first, key_last
    )
    return (layer_out[None], grad_query[None], grad_keys[None], grad_values[None], weight_grad)


def solution(mesh, n_y=Y_CHIPS):
    return jax.shard_map(
        functools.partial(body, mesh.shape["seq"], mesh.shape["dp"], n_y),
        mesh=mesh,
        in_specs=(
            P("dp", "seq", None),
            P("dp", "seq", None),
            P("dp", "seq", None),
            P("seq", None),
            P("dp", "seq", None),
            P("dp", "seq"),
            P("dp", "seq"),
        ),
        out_specs=(
            P("dp", "seq", None),
            P("dp", "seq", None),
            P("dp", "seq", None),
            P("dp", "seq", None),
            P("seq", None),
        ),
        check_vma=False,
    )
```

time: 408 us -> 115 us (0.28)
  local copies, waits for them, and re-layouts: 168 us -> 6.89 us
  Pallas kernels: 0 us -> 107 us
  matrix products: 96.1 us -> 0 us
  waiting for transfers between devices: 57.9 us -> 0 us
  other arithmetic: 46.3 us -> 0 us
  between operations: 21.7 us -> 0.66 us
  starting transfers between devices: 13.7 us -> 0 us
    pallas_call x0 -> x1, Pallas kernels: none -> 107 us  [body(): pl.pallas_call(functools.partial(kernel, sizes), out_shape=(jax.ShapeDtyp...]
    dot_general x8 -> x0, matrix products: 82 us -> none  [the longest x1 19.4 us: advance(): jnp.einsum('jhqk,jkhd->jqhd', grad_scores, key_tiles, preferred_element_t...]
    dynamic_update_slice x4 -> x0, local copies, waits for them, and re-layouts: 59.1 us -> none  [advance(): lax.dynamic_update_slice_in_dim(running, current + contributions[member],...]
    psum x1 -> x0, waiting for transfers between devices: 49.9 us -> none  [body(): summed = lax.psum(shard_sum.astype(jnp.bfloat16), 'dp').astype(jnp.float32)]
    gather x16 -> x0, local copies, waits for them, and re-layouts: 38.1 us -> none
    slice x8 -> x0, local copies, waits for them, and re-layouts: 30.4 us -> none  [the longest x2 13.5 us: advance(): value_tiles = kv_tiles[:, 1].reshape(4, window_rows, HEADS, HDIM)]
    add x4 -> x0, other arithmetic: 25.1 us -> none  [the longest x3 25.1 us: advance(): current + contributions[member]]
    reshape x3 -> x0, local copies, waits for them, and re-layouts: 23.7 us -> none  [the longest x2 22.9 us: advance(): contributions = jnp.stack([key_part, value_part], axis=1)]
  transfers between devices with their start and end apart: 7 -> 0, of which waited for: 3 -> 0; matrix products, arithmetic and copies ran while one was open for 76% -> 0% of each run, Pallas kernels for 0% -> 0%
where the time goes in v1:
time: 115 us
  Pallas kernels  107 us (93%)
  local copies, waits for them, and re-layouts  6.89 us (6%)
    pallas_call x1, Pallas kernels, body(): pl.pallas_call(functools.partial(kernel, sizes), out_shape=(jax.ShapeDtyp...  107 us
    unnamed x13, local copies, waits for them, and re-layouts  6.89 us

profile of v1, /device:TPU:1, one launch (start us, length us, event | category | flops | bytes accessed | tf_op | source)
XLA Modules:
  0.0 114.5 jit_solution(15658984034576438388)
XLA Ops:
  0.6 107.0 %shard_map.110 = (bf16[512,2048]{1,0:T(8,128)(2,1)}, bf16[512,1024]{1,0:T(8,128)(2,1)}, bf16[512,1024]{1,0:T(8,128)(2,1)}, bf16[512,1024]{1,0:T(8,128)(2,1)}, f32[16,2048]{1,0:T(8,128)}) custom-call(bf16[512,1024]{1,0:T(8,128)(2,1)} %bitcast.13, bf16[512,1024]{1,0:T(8,128)(2,1)} %bitcast.14, bf16[512,1024]{1,0:T(8,128)(2,1)} %bitcast.15, ...), custom_call_target="tpu_custom_call" | custom-call | tf_op jit(solution)/shard_map/pallas_call | solution.py:482
  107.6 0.0 copy-start.2
  107.6 0.0 copy-start.1
  107.6 3.3 %copy.17 = bf16[1,512,2048]{2,1,0:T(8,128)(2,1)} copy(bf16[1,512,2048]{2,1,0:T(8,128)(2,1)} %bitcast.9) | data formatting | bytes 4194304
  110.9 0.0 copy-done.2
  110.9 0.0 copy-start
  110.9 1.0 copy.18
  111.9 0.0 copy-done.1
  111.9 0.0 copy-start.3
  111.9 1.0 copy.19
  112.9 0.0 copy-done
  112.9 1.0 copy.20
  113.9 0.0 copy-done.3
  113.9 0.7 copy.21
Async XLA Ops:
  107.6 3.3 %copy-start.2 = (bf16[512,1024]{1,0:T(8,128)(2,1)S(1)}, bf16[512,1024]{1,0:T(8,128)(2,1)}, u32[]{:S(2)}) copy-start(bf16[512,1024]{1,0:T(8,128)(2,1)} %get-tuple-element.11) | copy-start | bytes 3145732
  107.6 4.3 %copy-start.1 = (bf16[512,1024]{1,0:T(8,128)(2,1)S(1)}, bf16[512,1024]{1,0:T(8,128)(2,1)}, u32[]{:S(2)}) copy-start(bf16[512,1024]{1,0:T(8,128)(2,1)} %get-tuple-element.12) | copy-start | bytes 3145732
  110.9 1.9 %copy-start = (bf16[512,1024]{1,0:T(8,128)(2,1)S(1)}, bf16[512,1024]{1,0:T(8,128)(2,1)}, u32[]{:S(2)}) copy-start(bf16[512,1024]{1,0:T(8,128)(2,1)} %get-tuple-element.13) | copy-start | bytes 3145732
  111.9 1.9 %copy-start.3 = (f32[16,2048]{1,0:T(8,128)S(1)}, f32[16,2048]{1,0:T(8,128)}, u32[]{:S(2)}) copy-start(f32[16,2048]{1,0:T(8,128)} %get-tuple-element.24) | copy-start | bytes 393220

commit v2 on v1

--- a/solution.py
+++ b/solution.py
@@ -28,12 +28,13 @@
     layer_hbm, dq_hbm, dk_hbm, dv_hbm, wgrad_hbm,
     w, q, kg, vg, go, probs, attn_t, attn, ga, bias,
     dq, dk_own, dv_own, dk_send, dv_send, dk_recv, dv_recv, layer,
-    wg, sib_recv, plus_send, plus_recv, minus_send, minus_recv,
+    wg, sib_recv, side_send, side_recv, plus_send, plus_recv, minus_send, minus_recv,
     z_sum, y_send, y_recv, x_all, wgrad,
     load_sem, store_sem,
     halo_send_sem, halo_recv_sem,
     agy_send_sem, agy_recv_sem, agp_send_sem, agp_recv_sem, agm_send_sem, agm_recv_sem,
-    ags_send_sem, ags_recv_sem,
+    agx_send_sem, agx_recv_sem, ags_send_sem, ags_recv_sem,
+    rsw_send_sem, rsw_recv_sem,
     rss_send_sem, rss_recv_sem, rsp_send_sem, rsp_recv_sem, rsm_send_sem, rsm_recv_sem,
     rsy_send_sem, rsy_recv_sem, rsx_send_sem, rsx_recv_sem,
     grad_send_sem, grad_recv_sem,
@@ -56,6 +57,13 @@
     z_prev = at_zy((z + n_z - 1) % n_z, y, c)
     y_peers = [at_zy(z, (y + j) % n_y, c) for j in range(1, n_y)]
     x_peers = [(x + j) % n_x for j in range(1, n_x)]
+    x_next, x_prev = (x + 1) % n_x, (x + n_x - 1) % n_x
+    half, quarter = width // 2, width // 4
+    mine, other = (x % 2) * half, (1 - x % 2) * half
+
+    def wide(start, size):
+        return pl.ds(pl.multiple_of(start, 128), size)
+
     partners = (sibling, across)
     group = (1 - c, c)
 
@@ -113,33 +121,49 @@
         for j, peer in enumerate(y_peers)
     ]
 
-    halo = []
+    hd = heads * HDIM
+    head_parts = ((0, heads // 2), (heads // 2, heads))
+
+    def part_cols(part):
+        low, high = head_parts[part]
+        return pl.ds(low * HDIM, (high - low) * HDIM)
+
+    halo = {}
     for t in (1, 0):
-        for which, (src, dst) in enumerate(((k_hbm, kg), (v_hbm, vg))):
-            halo.append(
-                send(
-                    src.at[token_rows(t)],
-                    dst.at[t, pl.ds(HALF, HALF)],
-                    halo_send_sem.at[t * 2 + which],
-                    halo_recv_sem.at[t * 2 + which],
-                    {"seq": partners[t]},
+        for part in range(2):
+            halo[t, part] = []
+            for which, (src, dst) in enumerate(((k_hbm, kg), (v_hbm, vg))):
+                i = (t * 2 + part) * 2 + which
+                halo[t, part].append(
+                    send(
+                        src.at[token_rows(t), part_cols(part)],
+                        dst.at[t, pl.ds(HALF, HALF), part_cols(part)],
+                        halo_send_sem.at[i],
+                        halo_recv_sem.at[i],
+                        {"seq": partners[t]},
+                    )
                 )
-            )
-    halo = {1: halo[:2], 0: halo[2:]}
-
-    def slab(z_index):
-        return w.at[pl.ds(z_index * n_y, n_y), c]
-
-    ag_sib = []
-
-    def share_slab(z_index):
+
+    def slab(z_index, start, size):
+        return w.at[pl.ds(z_index * n_y, n_y), c, :, wide(start, size)]
+
+    ag_sib, ag_side = [], {}
+
+    def share_slab(z_index, start, size):
         i = len(ag_sib)
+        piece = slab(z_index, start, size)
         ag_sib.append(
-            send(
-                slab(z_index), slab(z_index), ags_send_sem.at[i], ags_recv_sem.at[i],
-                {"seq": sibling},
-            )
-        )
+            send(piece, piece, ags_send_sem.at[i], ags_recv_sem.at[i], {"seq": sibling})
+        )
+
+    def pass_aside(z_index, key):
+        ag_side[key] = []
+        for start, peer in ((mine, x_next), (mine + quarter, x_prev)):
+            i = 2 * len(ag_side) - 2 + len(ag_side[key])
+            piece = slab(z_index, start, quarter)
+            ag_side[key].append(
+                send(piece, piece, agx_send_sem.at[i], agx_recv_sem.at[i], {"dp": peer})
+            )
 
     agp, agm = [], []
 
@@ -152,25 +176,32 @@
         if 0 < k <= n_plus:
             agp[k - 1].wait_recv()
         if k < n_plus:
+            piece = slab(from_prev, mine, half)
             agp.append(
-                send(
-                    slab(from_prev), slab(from_prev), agp_send_sem.at[k], agp_recv_sem.at[k],
-                    {"seq": z_next},
-                )
-            )
+                send(piece, piece, agp_send_sem.at[k], agp_recv_sem.at[k], {"seq": z_next})
+            )
+        if 0 < k <= n_plus:
+            pass_aside(from_prev, (1, k))
         if 0 < k <= n_minus:
             agm[k - 1].wait_recv()
         if k < n_minus:
+            piece = slab(from_next, mine, half)
             agm.append(
-                send(
-                    slab(from_next), slab(from_next), agm_send_sem.at[k], agm_recv_sem.at[k],
-                    {"seq": z_prev},
-                )
-            )
-        if k <= n_plus:
-            share_slab(from_prev)
+                send(piece, piece, agm_send_sem.at[k], agm_recv_sem.at[k], {"seq": z_prev})
+            )
         if 0 < k <= n_minus:
-            share_slab(from_next)
+            pass_aside(from_next, (-1, k))
+        if k == 0:
+            share_slab(z, 0, width)
+        if 0 < k <= n_plus:
+            share_slab(from_prev, mine, half)
+        if 0 < k <= n_minus:
+            share_slab(from_next, mine, half)
+        for way, last in ((1, n_plus), (-1, n_minus)):
+            if 1 <= k - 1 <= last:
+                for copy in ag_side[way, k - 1]:
+                    copy.wait_recv()
+                share_slab((z + n_z - way * (k - 1)) % n_z, other, half)
 
     for t in range(2):
         key_row = lax.broadcasted_iota(jnp.int32, (2 * HALF, HALF), 0)
@@ -191,11 +222,12 @@
     def columns(h):
         return pl.ds(pl.multiple_of(h * HDIM, HDIM), HDIM)
 
-    def forward(t):
-        load_q[t].wait()
-        load_k[t].wait()
-        load_v[t].wait()
-        for copy in halo[t]:
+    def forward(t, part):
+        if part == 0:
+            load_q[t].wait()
+            load_k[t].wait()
+            load_v[t].wait()
+        for copy in halo[t, part]:
             copy.wait_recv()
 
         def head(h, carry):
@@ -213,9 +245,11 @@
             attn[pl.ds(t * HALF, HALF), cols] = out_t.T.astype(BF16)
             return carry
 
-        lax.fori_loop(0, heads, head, 0)
-
-    def backward(t):
+        lax.fori_loop(*head_parts[part], head, 0)
+
+    grads = {}
+
+    def backward(t, part):
         def head(h, carry):
             cols = columns(h)
             p = probs[t, h]
@@ -233,37 +267,50 @@
             dv_send[t, :, cols] = dv[HALF:].astype(BF16)
             return carry
 
-        lax.fori_loop(0, heads, head, 0)
-        return [
-            send(
-                src.at[t], dst.at[t], grad_send_sem.at[2 * t + i], grad_recv_sem.at[2 * t + i],
-                {"seq": partners[t]},
-            )
-            for i, (src, dst) in enumerate(((dk_send, dk_recv), (dv_send, dv_recv)))
-        ]
+        lax.fori_loop(*head_parts[part], head, 0)
+        grads[t, part] = []
+        for which, (src, dst) in enumerate(((dk_send, dk_recv), (dv_send, dv_recv))):
+            i = (t * 2 + part) * 2 + which
+            grads[t, part].append(
+                send(
+                    src.at[t, :, part_cols(part)], dst.at[t, :, part_cols(part)],
+                    grad_send_sem.at[i], grad_recv_sem.at[i], {"seq": partners[t]},
+                )
+            )
 
     ag_step(0)
-    forward(0)
+    forward(0, 0)
     ag_step(1)
-    forward(1)
-    if n_plus >= 2:
-        ag_step(2)
+    forward(0, 1)
+    ag_step(2)
+    forward(1, 0)
+    for k in range(3, n_plus + 1):
+        ag_step(k)
+    forward(1, 1)
+    ag_step(n_plus + 1)
 
     for copy in load_go:
         copy.wait()
-    hd = heads * HDIM
     row_blocks, col_width = hd // HALF, min(512, width)
 
-    def weight_tile(i, carry):
-        r, n = i % row_blocks, i // row_blocks
-        cols = pl.ds(pl.multiple_of(n * col_width, col_width), col_width)
+    def weight_rows(i):
+        r = (z * row_blocks // n_z + row_blocks // 2 + i) % row_blocks
         left = attn_t[pl.ds(pl.multiple_of(r * HALF, HALF), HALF), :]
-        right = go[:, :, cols].reshape(2 * HALF, col_width)
-        tile = dot(left, right, ((1,), (0,))).astype(BF16)
-        wg[pl.ds(r * 8, 8), :, :, cols] = tile.reshape(8, CORES, 16, col_width)
-        return carry
-
-    lax.fori_loop(0, row_blocks * (width // col_width), weight_tile, 0)
+
+        def tile(n, carry):
+            cols = wide(n * col_width, col_width)
+            right = go[:, :, cols].reshape(2 * HALF, col_width)
+            block = dot(left, right, ((1,), (0,))).astype(BF16)
+            wg[pl.ds(r * 8, 8), :, :, cols] = block.reshape(8, CORES, 16, col_width)
+            return carry
+
+        lax.fori_loop(0, width // col_width, tile, 0)
+        return send(
+            wg.at[pl.ds(r * 8, 8), 1 - c], sib_recv.at[pl.ds(r * 8, 8)], rss_send_sem.at[i],
+            rss_recv_sem.at[i], {"seq": sibling},
+        )
+
+    rss = [weight_rows(i) for i in range(row_blocks)]
 
     order = []
     for k in range(max(n_plus, n_minus), 0, -1):
@@ -272,19 +319,37 @@
         if k <= n_minus:
             order.append((-1, k))
     order.append((1, 0))
-    rss = {}
+    for copy in rss:
+        copy.wait_recv()
+    rsw = []
     for i, (way, k) in enumerate(order):
-        d = (z + way * k + n_z) % n_z
-        rss[way, k] = send(
-            wg.at[pl.ds(d * n_y, n_y), 1 - c], sib_recv.at[i], rss_send_sem.at[i],
-            rss_recv_sem.at[i], {"seq": sibling},
+        first_row = (z + way * k + n_z) % n_z * n_y
+
+        def add_cores(j, carry, i=i, first_row=first_row):
+            for part in range(2):
+                cols = wide(other + part * quarter, quarter)
+                total = wg[first_row + j, c, :, cols].astype(F32)
+                total = total + sib_recv[first_row + j, :, cols].astype(F32)
+                side_send[i, part, j] = total.astype(BF16)
+            return carry
+
+        lax.fori_loop(0, n_y, add_cores, 0)
+        rsw.append(
+            [
+                send(
+                    side_send.at[i, part], side_recv.at[i, part], rsw_send_sem.at[2 * i + part],
+                    rsw_recv_sem.at[2 * i + part], {"dp": peer},
+                )
+                for part, peer in enumerate((x_next, x_prev))
+            ]
         )
     rsp, rsm = {}, {}
 
     def chain(way, k):
         i = order.index((way, k))
-        d = (z + way * k + n_z) % n_z
-        rss[way, k].wait_recv()
+        first_row = (z + way * k + n_z) % n_z * n_y
+        for copy in rsw[i]:
+            copy.wait_recv()
         arrivals = []
         if (way == 1 or k == 0) and k < n_plus:
             rsp[k + 1].wait_recv()
@@ -294,16 +359,21 @@
             arrivals.append(minus_recv)
 
         def add(j, carry):
-            total = wg[d * n_y + j, c].astype(F32) + sib_recv[i, j].astype(F32)
-            for ref in arrivals:
-                total = total + ref[k, j].astype(F32)
-            if k == 0:
-                z_sum[j] = total
-                y_send[j] = total.astype(BF16)
-            elif way == 1:
-                plus_send[k - 1, j] = total.astype(BF16)
-            else:
-                minus_send[k - 1, j] = total.astype(BF16)
+            for part in range(2):
+                cols = wide(mine + part * quarter, quarter)
+                here = pl.ds(part * quarter, quarter)
+                total = wg[first_row + j, c, :, cols].astype(F32)
+                total = total + sib_recv[first_row + j, :, cols].astype(F32)
+                total = total + side_recv[i, part, j].astype(F32)
+                for ref in arrivals:
+                    total = total + ref[k, j, :, here].astype(F32)
+                if k == 0:
+                    z_sum[j, :, here] = total
+                    y_send[j, :, here] = total.astype(BF16)
+                elif way == 1:
+                    plus_send[k - 1, j, :, here] = total.astype(BF16)
+                else:
+                    minus_send[k - 1, j, :, here] = total.astype(BF16)
             return carry
 
         lax.fori_loop(0, n_y, add, 0)
@@ -324,9 +394,6 @@
         if 0 < k <= n_minus:
             chain(-1, k)
 
-    chain_level(n_plus)
-    for k in range(3, n_plus + 1):
-        ag_step(k)
     for copy in ag_sib:
         copy.wait_recv()
 
@@ -338,16 +405,13 @@
 
     lax.fori_loop(0, row_blocks, grad_tile, 0)
 
-    levels = list(range(n_plus - 1, 0, -1))
-    grads = {}
-    if levels:
-        chain_level(levels.pop(0))
-    grads[1] = backward(1)
-    if levels:
-        chain_level(levels.pop(0))
-    grads[0] = backward(0)
-    for k in levels:
+    steps = [(1, 0), (1, 1), (0, 0), (0, 1)]
+    for k in range(n_plus, 0, -1):
         chain_level(k)
+        if steps:
+            backward(*steps.pop(0))
+    for step in steps:
+        backward(*step)
     chain_level(0)
 
     stores = []
@@ -393,7 +457,7 @@
         store(layer.at[pl.ds(t * HALF, HALF)], layer_hbm.at[token_rows(t)])
 
     for t in (0, 1):
-        for copy in grads[t]:
+        for copy in grads[t, 0] + grads[t, 1]:
             copy.wait()
         for own, got, out, hbm in (
             (dk_own, dk_recv, dk_send, dk_hbm), (dv_own, dv_recv, dv_send, dv_hbm)
@@ -408,13 +472,14 @@
 
     for copy in rsx:
         copy.wait_recv()
-    total = x_all[0].astype(F32)
-    for j in range(1, n_x):
-        total = total + x_all[j].astype(F32)
-    wgrad[...] = total * (1.0 / norm)
+    for parity in range(2):
+        total = x_all[parity].astype(F32)
+        for j in range(parity + 2, n_x, 2):
+            total = total + x_all[j].astype(F32)
+        wgrad[:, pl.ds(parity * half, half)] = total * (1.0 / norm)
     store(wgrad, wgrad_hbm)
 
-    waited = grads[0] + grads[1]
+    waited = sum(grads.values(), [])
     for copy in sent:
         if not any(copy is other for other in waited):
             copy.wait_send()
@@ -453,29 +518,33 @@
         vmem((2, HALF, hd), BF16),
         vmem((2 * HALF, width), BF16),
         vmem((n_zy, CORES, 16, width), BF16),
-        vmem((n_z, n_y, 16, width), BF16),
-        vmem((n_plus, n_y, 16, width), BF16),
-        vmem((n_plus, n_y, 16, width), BF16),
-        vmem((max(n_minus, 1), n_y, 16, width), BF16),
-        vmem((max(n_minus, 1), n_y, 16, width), BF16),
-        vmem((n_y, 16, width), F32),
-        vmem((n_y, 16, width), BF16),
-        vmem((n_y - 1, 16, width), BF16),
-        vmem((n_x, 16, width), BF16),
+        vmem((n_zy, 16, width), BF16),
+        vmem((n_z, 2, n_y, 16, width // 4), BF16),
+        vmem((n_z, 2, n_y, 16, width // 4), BF16),
+        vmem((n_plus, n_y, 16, width // 2), BF16),
+        vmem((n_plus, n_y, 16, width // 2), BF16),
+        vmem((max(n_minus, 1), n_y, 16, width // 2), BF16),
+        vmem((max(n_minus, 1), n_y, 16, width // 2), BF16),
+        vmem((n_y, 16, width // 2), F32),
+        vmem((n_y, 16, width // 2), BF16),
+        vmem((n_y - 1, 16, width // 2), BF16),
+        vmem((n_x, 16, width // 2), BF16),
         vmem((16, width), F32),
         dma((9,)),
         dma((9,)),
-        dma((4,)), dma((4,)),
+        dma((8,)), dma((8,)),
         dma((n_y - 1,)), dma((n_y - 1,)),
         dma((n_plus,)), dma((n_plus,)),
         dma((max(n_minus, 1),)), dma((max(n_minus, 1),)),
-        dma((n_z,)), dma((n_z,)),
-        dma((n_z,)), dma((n_z,)),
+        dma((2 * n_z,)), dma((2 * n_z,)),
+        dma((2 * n_z,)), dma((2 * n_z,)),
+        dma((2 * n_z,)), dma((2 * n_z,)),
+        dma((hd // HALF,)), dma((hd // HALF,)),
         dma((n_plus,)), dma((n_plus,)),
         dma((max(n_minus, 1),)), dma((max(n_minus, 1),)),
         dma((n_y - 1,)), dma((n_y - 1,)),
         dma((n_x - 1,)), dma((n_x - 1,)),
-        dma((4,)), dma((4,)),
+        dma((8,)), dma((8,)),
     ]
     hbm = pl.BlockSpec(memory_space=pl.ANY)
     smem = pl.BlockSpec(memory_space=pltpu.SMEM)

time: 115 us -> 102 us (0.89)
  Pallas kernels: 107 us -> 94.3 us
    pallas_call x1, Pallas kernels: 107 us -> 94.3 us  [body(): pl.pallas_call(functools.partial(kernel, sizes), out_shape=(jax.ShapeDtyp...]
where the time goes in v2:
time: 102 us
  Pallas kernels  94.3 us (92%)
  local copies, waits for them, and re-layouts  6.89 us (7%)
    pallas_call x1, Pallas kernels, body(): pl.pallas_call(functools.partial(kernel, sizes), out_shape=(jax.ShapeDtyp...  94.3 us
    unnamed x13, local copies, waits for them, and re-layouts  6.89 us

profile of v2, /device:TPU:1, one launch (start us, length us, event | category | flops | bytes accessed | tf_op | source)
XLA Modules:
  0.0 101.8 jit_solution(17821711189917758777)
XLA Ops:
  0.6 94.3 %shard_map.110 = (bf16[512,2048]{1,0:T(8,128)(2,1)}, bf16[512,1024]{1,0:T(8,128)(2,1)}, bf16[512,1024]{1,0:T(8,128)(2,1)}, bf16[512,1024]{1,0:T(8,128)(2,1)}, f32[16,2048]{1,0:T(8,128)}) custom-call(bf16[512,1024]{1,0:T(8,128)(2,1)} %bitcast.13, bf16[512,1024]{1,0:T(8,128)(2,1)} %bitcast.14, bf16[512,1024]{1,0:T(8,128)(2,1)} %bitcast.15, ...), custom_call_target="tpu_custom_call" | custom-call | tf_op jit(solution)/shard_map/pallas_call | solution.py:551
  94.9 0.0 copy-start.2
  94.9 0.0 copy-start.1
  94.9 3.3 %copy.17 = bf16[1,512,2048]{2,1,0:T(8,128)(2,1)} copy(bf16[1,512,2048]{2,1,0:T(8,128)(2,1)} %bitcast.9) | data formatting | bytes 4194304
  98.2 0.0 copy-done.2
  98.2 0.0 copy-start
  98.2 1.0 copy.18
  99.2 0.0 copy-done.1
  99.2 0.0 copy-start.3
  99.2 1.0 copy.19
  100.2 0.0 copy-done
  100.2 1.0 copy.20
  101.1 0.0 copy-done.3
  101.1 0.7 copy.21
Async XLA Ops:
  94.9 3.3 %copy-start.2 = (bf16[512,1024]{1,0:T(8,128)(2,1)S(1)}, bf16[512,1024]{1,0:T(8,128)(2,1)}, u32[]{:S(2)}) copy-start(bf16[512,1024]{1,0:T(8,128)(2,1)} %get-tuple-element.11) | copy-start | bytes 3145732
  94.9 4.3 %copy-start.1 = (bf16[512,1024]{1,0:T(8,128)(2,1)S(1)}, bf16[512,1024]{1,0:T(8,128)(2,1)}, u32[]{:S(2)}) copy-start(bf16[512,1024]{1,0:T(8,128)(2,1)} %get-tuple-element.12) | copy-start | bytes 3145732
  98.2 1.9 %copy-start = (bf16[512,1024]{1,0:T(8,128)(2,1)S(1)}, bf16[512,1024]{1,0:T(8,128)(2,1)}, u32[]{:S(2)}) copy-start(bf16[512,1024]{1,0:T(8,128)(2,1)} %get-tuple-element.13) | copy-start | bytes 3145732
  99.2 1.9 %copy-start.3 = (f32[16,2048]{1,0:T(8,128)S(1)}, f32[16,2048]{1,0:T(8,128)}, u32[]{:S(2)}) copy-start(f32[16,2048]{1,0:T(8,128)} %get-tuple-element.24) | copy-start | bytes 393220

commit v3 on v2

--- a/solution.py
+++ b/solution.py
@@ -16,6 +16,15 @@
 F32 = jnp.float32
 BF16 = jnp.bfloat16
 NEVER = -1e30
+PLAN = (
+    "ag0 f00 f01 f10", "wg0 ag1 f11 f02", "wg1 xs0 f03 ag2", "f12 wg2 xs1 zs4",
+    "f13 wg3 xs2 ag3", "zs3 ga0 b10 xs3", "zs2 b00 ag4 ga1", "b11 zs1 b01 ga2",
+    "b12 zs0 b02 ag5", "ga3 b13 b03",
+)
+SMALL_PLAN = (
+    "ag0 f00 f10 wg0", "ag1 f01 xs0 ag2", "f11 wg1 ga0 zs2", "xs1 b10 b00 zs1",
+    "ag3 ga1 b11 zs0", "b01",
+)
 
 
 def dot(a, b, dims):
@@ -64,6 +73,15 @@
     def wide(start, size):
         return pl.ds(pl.multiple_of(start, 128), size)
 
+    pairs = n_z // 2
+
+    def near_first(z_index):
+        side = 2 * (z_index % 2) - 1
+        steps = (0, side, -side, 2)[:pairs]
+        return [(z_index // 2 + step + pairs) % pairs for step in steps]
+
+    near, far = near_first(z), near_first(z)[::-1]
+
     partners = (sibling, across)
     group = (1 - c, c)
 
@@ -121,25 +139,22 @@
         for j, peer in enumerate(y_peers)
     ]
 
-    hd = heads * HDIM
-    head_parts = ((0, heads // 2), (heads // 2, heads))
-
-    def part_cols(part):
-        low, high = head_parts[part]
-        return pl.ds(low * HDIM, (high - low) * HDIM)
+    def pair_cols(r):
+        return pl.ds(pl.multiple_of(r * HALF, HALF), HALF)
 
     halo = {}
     for t in (1, 0):
-        for part in range(2):
-            halo[t, part] = []
+        partner_far = near_first(partners[t] // CORES // n_y)[::-1]
+        for i, r in enumerate(partner_far):
+            halo[t, i] = []
             for which, (src, dst) in enumerate(((k_hbm, kg), (v_hbm, vg))):
-                i = (t * 2 + part) * 2 + which
-                halo[t, part].append(
+                n = (t * pairs + i) * 2 + which
+                halo[t, i].append(
                     send(
-                        src.at[token_rows(t), part_cols(part)],
-                        dst.at[t, pl.ds(HALF, HALF), part_cols(part)],
-                        halo_send_sem.at[i],
-                        halo_recv_sem.at[i],
+                        src.at[token_rows(t), pair_cols(r)],
+                        dst.at[t, pl.ds(HALF, HALF), pair_cols(r)],
+                        halo_send_sem.at[n],
+                        halo_recv_sem.at[n],
                         {"seq": partners[t]},
                     )
                 )
@@ -147,13 +162,13 @@
     def slab(z_index, start, size):
         return w.at[pl.ds(z_index * n_y, n_y), c, :, wide(start, size)]
 
-    ag_sib, ag_side = [], {}
-
-    def share_slab(z_index, start, size):
+    ag_sib, ag_side = {}, {}
+
+    def share_slab(key, z_index, start, size):
         i = len(ag_sib)
         piece = slab(z_index, start, size)
-        ag_sib.append(
-            send(piece, piece, ags_send_sem.at[i], ags_recv_sem.at[i], {"seq": sibling})
+        ag_sib[key] = send(
+            piece, piece, ags_send_sem.at[i], ags_recv_sem.at[i], {"seq": sibling}
         )
 
     def pass_aside(z_index, key):
@@ -192,16 +207,16 @@
         if 0 < k <= n_minus:
             pass_aside(from_next, (-1, k))
         if k == 0:
-            share_slab(z, 0, width)
+            share_slab((0, 0), z, 0, width)
         if 0 < k <= n_plus:
-            share_slab(from_prev, mine, half)
+            share_slab((1, k), from_prev, mine, half)
         if 0 < k <= n_minus:
-            share_slab(from_next, mine, half)
+            share_slab((-1, k), from_next, mine, half)
         for way, last in ((1, n_plus), (-1, n_minus)):
             if 1 <= k - 1 <= last:
                 for copy in ag_side[way, k - 1]:
                     copy.wait_recv()
-                share_slab((z + n_z - way * (k - 1)) % n_z, other, half)
+                share_slab((way, k - 1, 1), (z + n_z - way * (k - 1)) % n_z, other, half)
 
     for t in range(2):
         key_row = lax.broadcasted_iota(jnp.int32, (2 * HALF, HALF), 0)
@@ -219,19 +234,15 @@
         inside = (key_block >= lower) & (key_block < upper)
         bias[t] = jnp.where(inside, 0.0, NEVER)
 
-    def columns(h):
-        return pl.ds(pl.multiple_of(h * HDIM, HDIM), HDIM)
-
-    def forward(t, part):
-        if part == 0:
+    def forward(t, i):
+        if i == 0:
             load_q[t].wait()
             load_k[t].wait()
             load_v[t].wait()
-        for copy in halo[t, part]:
+        for copy in halo[t, i]:
             copy.wait_recv()
-
-        def head(h, carry):
-            cols = columns(h)
+        for h in (2 * far[i], 2 * far[i] + 1):
+            cols = wide(h * HDIM, HDIM)
             scores = dot(kg[t, :, cols], q[t, :, cols], ((1,), (1,))) * scale + bias[t]
             highest = jnp.max(scores, axis=0, keepdims=True)
             raised = jnp.exp(scores - highest)
@@ -239,19 +250,14 @@
             p = raised * (1.0 / total)
             probs[t, h] = p
             out_t = dot(vg[t, :, cols], p.astype(BF16), ((0,), (0,)))
-            attn_t[pl.ds(pl.multiple_of(h * HDIM, HDIM), HDIM), pl.ds(t * HALF, HALF)] = (
-                out_t.astype(BF16)
-            )
+            attn_t[cols, pl.ds(t * HALF, HALF)] = out_t.astype(BF16)
             attn[pl.ds(t * HALF, HALF), cols] = out_t.T.astype(BF16)
-            return carry
-
-        lax.fori_loop(*head_parts[part], head, 0)
-
-    grads = {}
-
-    def backward(t, part):
-        def head(h, carry):
-            cols = columns(h)
+
+    grads = []
+
+    def backward(t, i):
+        for h in (2 * near[i], 2 * near[i] + 1):
+            cols = wide(h * HDIM, HDIM)
             p = probs[t, h]
             grad_rows = ga[pl.ds(t * HALF, HALF), cols]
             grad_p = dot(vg[t, :, cols], grad_rows, ((1,), (1,)))
@@ -265,37 +271,24 @@
             dv_own[t, :, cols] = dv[:HALF]
             dk_send[t, :, cols] = dk[HALF:].astype(BF16)
             dv_send[t, :, cols] = dv[HALF:].astype(BF16)
-            return carry
-
-        lax.fori_loop(*head_parts[part], head, 0)
-        grads[t, part] = []
         for which, (src, dst) in enumerate(((dk_send, dk_recv), (dv_send, dv_recv))):
-            i = (t * 2 + part) * 2 + which
-            grads[t, part].append(
-                send(
-                    src.at[t, :, part_cols(part)], dst.at[t, :, part_cols(part)],
-                    grad_send_sem.at[i], grad_recv_sem.at[i], {"seq": partners[t]},
-                )
-            )
-
-    ag_step(0)
-    forward(0, 0)
-    ag_step(1)
-    forward(0, 1)
-    ag_step(2)
-    forward(1, 0)
-    for k in range(3, n_plus + 1):
-        ag_step(k)
-    forward(1, 1)
-    ag_step(n_plus + 1)
-
-    for copy in load_go:
-        copy.wait()
-    row_blocks, col_width = hd // HALF, min(512, width)
+            n = (t * pairs + i) * 2 + which
+            piece = pair_cols(near[i])
+            copy = send(
+                src.at[t, :, piece], dst.at[t, :, piece], grad_send_sem.at[n],
+                grad_recv_sem.at[n], {"seq": partners[t]},
+            )
+            grads.append((copy, t))
+
+    hd = heads * HDIM
+    col_width = min(512, width)
 
     def weight_rows(i):
-        r = (z * row_blocks // n_z + row_blocks // 2 + i) % row_blocks
-        left = attn_t[pl.ds(pl.multiple_of(r * HALF, HALF), HALF), :]
+        r = far[i]
+        if i == 0:
+            for copy in load_go:
+                copy.wait()
+        left = attn_t[pair_cols(r), :]
 
         def tile(n, carry):
             cols = wide(n * col_width, col_width)
@@ -305,27 +298,35 @@
             return carry
 
         lax.fori_loop(0, width // col_width, tile, 0)
-        return send(
-            wg.at[pl.ds(r * 8, 8), 1 - c], sib_recv.at[pl.ds(r * 8, 8)], rss_send_sem.at[i],
-            rss_recv_sem.at[i], {"seq": sibling},
-        )
-
-    rss = [weight_rows(i) for i in range(row_blocks)]
-
-    order = []
-    for k in range(max(n_plus, n_minus), 0, -1):
-        if k <= n_plus:
-            order.append((1, k))
-        if k <= n_minus:
-            order.append((-1, k))
-    order.append((1, 0))
-    for copy in rss:
-        copy.wait_recv()
-    rsw = []
-    for i, (way, k) in enumerate(order):
+        rss.append(
+            send(
+                wg.at[pl.ds(r * 8, 8), 1 - c], sib_recv.at[pl.ds(r * 8, 8)], rss_send_sem.at[i],
+                rss_recv_sem.at[i], {"seq": sibling},
+            )
+        )
+
+    def grad_attn(i):
+        for k in range(i + 2):
+            for way in (1, -1):
+                for key in ((way, k), (way, k, 1)):
+                    if key in ag_sib and key not in ag_here:
+                        ag_sib[key].wait_recv()
+                        ag_here.append(key)
+        if i == 0:
+            ag_sib[0, 0].wait_recv()
+        rows = w[pl.ds(near[i] * 8, 8)].reshape(HALF, width)
+        tile = dot(go[...].reshape(2 * HALF, width), rows, ((1,), (1,)))
+        ga[:, pair_cols(near[i])] = tile.astype(BF16)
+
+    rss, ag_here = [], []
+
+    rsw = {}
+
+    def aside(way, k):
+        i = len(rsw)
         first_row = (z + way * k + n_z) % n_z * n_y
 
-        def add_cores(j, carry, i=i, first_row=first_row):
+        def add_cores(j, carry):
             for part in range(2):
                 cols = wide(other + part * quarter, quarter)
                 total = wg[first_row + j, c, :, cols].astype(F32)
@@ -334,21 +335,29 @@
             return carry
 
         lax.fori_loop(0, n_y, add_cores, 0)
-        rsw.append(
-            [
-                send(
-                    side_send.at[i, part], side_recv.at[i, part], rsw_send_sem.at[2 * i + part],
-                    rsw_recv_sem.at[2 * i + part], {"dp": peer},
-                )
-                for part, peer in enumerate((x_next, x_prev))
-            ]
-        )
+        rsw[way, k] = i, [
+            send(
+                side_send.at[i, part], side_recv.at[i, part], rsw_send_sem.at[2 * i + part],
+                rsw_recv_sem.at[2 * i + part], {"dp": peer},
+            )
+            for part, peer in enumerate((x_next, x_prev))
+        ]
+
+    def aside_level(level):
+        rss[level].wait_recv()
+        k = n_plus - level
+        aside(1, k)
+        if k <= n_minus:
+            aside(-1, k)
+        if k == 1:
+            aside(1, 0)
+
     rsp, rsm = {}, {}
 
     def chain(way, k):
-        i = order.index((way, k))
+        i, copies = rsw[way, k]
         first_row = (z + way * k + n_z) % n_z * n_y
-        for copy in rsw[i]:
+        for copy in copies:
             copy.wait_recv()
         arrivals = []
         if (way == 1 or k == 0) and k < n_plus:
@@ -394,25 +403,14 @@
         if 0 < k <= n_minus:
             chain(-1, k)
 
-    for copy in ag_sib:
-        copy.wait_recv()
-
-    def grad_tile(i, carry):
-        rows = w[pl.ds(i * 8, 8)].reshape(HALF, width)
-        tile = dot(go[...].reshape(2 * HALF, width), rows, ((1,), (1,)))
-        ga[:, pl.ds(pl.multiple_of(i * HALF, HALF), HALF)] = tile.astype(BF16)
-        return carry
-
-    lax.fori_loop(0, row_blocks, grad_tile, 0)
-
-    steps = [(1, 0), (1, 1), (0, 0), (0, 1)]
-    for k in range(n_plus, 0, -1):
-        chain_level(k)
-        if steps:
-            backward(*steps.pop(0))
-    for step in steps:
-        backward(*step)
-    chain_level(0)
+    plan = PLAN if n_z == 8 else SMALL_PLAN
+    steps = {
+        "ag": ag_step, "f0": functools.partial(forward, 0), "f1": functools.partial(forward, 1),
+        "wg": weight_rows, "xs": aside_level, "zs": chain_level, "ga": grad_attn,
+        "b0": functools.partial(backward, 0), "b1": functools.partial(backward, 1),
+    }
+    for item in " ".join(plan).split():
+        steps[item[:2]](int(item[2:]))
 
     stores = []
 
@@ -456,8 +454,9 @@
     for t in range(2):
         store(layer.at[pl.ds(t * HALF, HALF)], layer_hbm.at[token_rows(t)])
 
+    grads_of = {t: [copy for copy, slot in grads if slot == t] for t in range(2)}
     for t in (0, 1):
-        for copy in grads[t, 0] + grads[t, 1]:
+        for copy in grads_of[t]:
             copy.wait()
         for own, got, out, hbm in (
             (dk_own, dk_recv, dk_send, dk_hbm), (dv_own, dv_recv, dv_send, dv_hbm)
@@ -479,7 +478,7 @@
         wgrad[:, pl.ds(parity * half, half)] = total * (1.0 / norm)
     store(wgrad, wgrad_hbm)
 
-    waited = sum(grads.values(), [])
+    waited = [copy for copy, _ in grads]
     for copy in sent:
         if not any(copy is other for other in waited):
             copy.wait_send()
@@ -532,7 +531,7 @@
         vmem((16, width), F32),
         dma((9,)),
         dma((9,)),
-        dma((8,)), dma((8,)),
+        dma((2 * n_z,)), dma((2 * n_z,)),
         dma((n_y - 1,)), dma((n_y - 1,)),
         dma((n_plus,)), dma((n_plus,)),
         dma((max(n_minus, 1),)), dma((max(n_minus, 1),)),
@@ -544,7 +543,7 @@
         dma((max(n_minus, 1),)), dma((max(n_minus, 1),)),
         dma((n_y - 1,)), dma((n_y - 1,)),
         dma((n_x - 1,)), dma((n_x - 1,)),
-        dma((8,)), dma((8,)),
+        dma((2 * n_z,)), dma((2 * n_z,)),
     ]
     hbm = pl.BlockSpec(memory_space=pl.ANY)
     smem = pl.BlockSpec(memory_space=pltpu.SMEM)

time: 102 us -> 87.8 us (0.86)
  Pallas kernels: 94.3 us -> 80.2 us
    pallas_call x1, Pallas kernels: 94.3 us -> 80.2 us  [body(): pl.pallas_call(functools.partial(kernel, sizes), out_shape=(jax.ShapeDtyp...]
where the time goes in v3:
time: 87.8 us; the launch traced here: 87.7 us
  Pallas kernels  80.2 us (91%)
  local copies, waits for them, and re-layouts  6.89 us (8%)
    pallas_call x1, Pallas kernels, body(): pl.pallas_call(functools.partial(kernel, sizes), out_shape=(jax.ShapeDtyp...  80.2 us
    unnamed x13, local copies, waits for them, and re-layouts  6.89 us

profile of v3, /device:TPU:1, one launch (start us, length us, event | category | flops | bytes accessed | tf_op | source)
XLA Modules:
  0.0 87.7 jit_solution(11280228539516914689)
XLA Ops:
  0.6 80.2 %shard_map.110 = (bf16[512,2048]{1,0:T(8,128)(2,1)}, bf16[512,1024]{1,0:T(8,128)(2,1)}, bf16[512,1024]{1,0:T(8,128)(2,1)}, bf16[512,1024]{1,0:T(8,128)(2,1)}, f32[16,2048]{1,0:T(8,128)}) custom-call(bf16[512,1024]{1,0:T(8,128)(2,1)} %bitcast.13, bf16[512,1024]{1,0:T(8,128)(2,1)} %bitcast.14, bf16[512,1024]{1,0:T(8,128)(2,1)} %bitcast.15, ...), custom_call_target="tpu_custom_call" | custom-call | tf_op jit(solution)/shard_map/pallas_call | solution.py:550
  80.8 0.0 copy-start.2
  80.8 0.0 copy-start.1
  80.8 3.3 %copy.17 = bf16[1,512,2048]{2,1,0:T(8,128)(2,1)} copy(bf16[1,512,2048]{2,1,0:T(8,128)(2,1)} %bitcast.9) | data formatting | bytes 4194304
  84.1 0.0 copy-done.2
  84.1 0.0 copy-start
  84.1 1.0 %copy.18 = bf16[1,512,1024]{2,1,0:T(8,128)(2,1)} copy(bf16[1,512,1024]{2,1,0:T(8,128)(2,1)S(1)} %bitcast.12) | data formatting | bytes 2097152
  85.1 0.0 copy-done.1
  85.1 0.0 copy-start.3
  85.1 1.0 %copy.19 = bf16[1,512,1024]{2,1,0:T(8,128)(2,1)} copy(bf16[1,512,1024]{2,1,0:T(8,128)(2,1)S(1)} %bitcast.11) | data formatting | bytes 2097152
  86.1 0.0 copy-done
  86.1 1.0 %copy.20 = bf16[1,512,1024]{2,1,0:T(8,128)(2,1)} copy(bf16[1,512,1024]{2,1,0:T(8,128)(2,1)S(1)} %bitcast.10) | data formatting | bytes 2097152
  87.1 0.0 copy-done.3
  87.1 0.7 copy.21
Async XLA Ops:
  80.8 3.3 %copy-start.2 = (bf16[512,1024]{1,0:T(8,128)(2,1)S(1)}, bf16[512,1024]{1,0:T(8,128)(2,1)}, u32[]{:S(2)}) copy-start(bf16[512,1024]{1,0:T(8,128)(2,1)} %get-tuple-element.11) | copy-start | bytes 3145732
  80.8 4.3 %copy-start.1 = (bf16[512,1024]{1,0:T(8,128)(2,1)S(1)}, bf16[512,1024]{1,0:T(8,128)(2,1)}, u32[]{:S(2)}) copy-start(bf16[512,1024]{1,0:T(8,128)(2,1)} %get-tuple-element.12) | copy-start | bytes 3145732
  84.1 1.9 %copy-start = (bf16[512,1024]{1,0:T(8,128)(2,1)S(1)}, bf16[512,1024]{1,0:T(8,128)(2,1)}, u32[]{:S(2)}) copy-start(bf16[512,1024]{1,0:T(8,128)(2,1)} %get-tuple-element.13) | copy-start | bytes 3145732
  85.1 1.9 %copy-start.3 = (f32[16,2048]{1,0:T(8,128)S(1)}, f32[16,2048]{1,0:T(8,128)}, u32[]{:S(2)}) copy-start(f32[16,2048]{1,0:T(8,128)} %get-tuple-element.24) | copy-start | bytes 393220

commit v4 on v3

--- a/solution.py
+++ b/solution.py
@@ -16,14 +16,15 @@
 F32 = jnp.float32
 BF16 = jnp.bfloat16
 NEVER = -1e30
+LAYER_PARTS = 4
 PLAN = (
-    "ag0 f00 f01 f10", "wg0 ag1 f11 f02", "wg1 xs0 f03 ag2", "f12 wg2 xs1 zs4",
-    "f13 wg3 xs2 ag3", "zs3 ga0 b10 xs3", "zs2 b00 ag4 ga1", "b11 zs1 b01 ga2",
-    "b12 zs0 b02 ag5", "ga3 b13 b03",
+    "ag0 f00 f01 f10", "wg0 ag1 f11 f02", "wg1 xs0 f03 f12", "ag2 wg2 xs1 zs4",
+    "f13 wg3 xs2 ag3", "ga0 zs3 b10 xs3", "b00 zs2 ag4 ga1", "b11 b01 zs1 ga2",
+    "b12 b02 ag5 zs0", "ys0 ga3 kp0 b13", "yx0 b03 xx0 gs0", "gs1",
 )
 SMALL_PLAN = (
     "ag0 f00 f10 wg0", "ag1 f01 xs0 ag2", "f11 wg1 ga0 zs2", "xs1 b10 b00 zs1",
-    "ag3 ga1 b11 zs0", "b01",
+    "ag3 ga1 kp0 b11", "zs0 ys0 b01 yx0", "gs0 gs1 xx0",
 )
 
 
@@ -34,9 +35,9 @@
 def kernel(
     sizes,
     q_hbm, k_hbm, v_hbm, shard_hbm, go_hbm, first_ref, last_ref,
-    layer_hbm, dq_hbm, dk_hbm, dv_hbm, wgrad_hbm,
+    attn_hbm, w_hbm, dq_hbm, dk_hbm, dv_hbm, wgrad_hbm,
     w, q, kg, vg, go, probs, attn_t, attn, ga, bias,
-    dq, dk_own, dv_own, dk_send, dv_send, dk_recv, dv_recv, layer,
+    dq, dk_own, dv_own, dk_send, dv_send, dk_recv, dv_recv,
     wg, sib_recv, side_send, side_recv, plus_send, plus_recv, minus_send, minus_recv,
     z_sum, y_send, y_recv, x_all, wgrad,
     load_sem, store_sem,
@@ -403,85 +404,127 @@
         if 0 < k <= n_minus:
             chain(-1, k)
 
+    stores = []
+
+    def store(src, dst):
+        copy = pltpu.make_async_copy(src, dst, store_sem.at[len(stores)])
+        copy.start()
+        stores.append(copy)
+
+    rsy, rsx = [], []
+
+    def along_y(_):
+        for j, peer in enumerate(y_peers, 1):
+            rsy.append(
+                send(
+                    y_send.at[(y + j) % n_y], y_recv.at[j - 1], rsy_send_sem.at[j - 1],
+                    rsy_recv_sem.at[j - 1], {"seq": peer},
+                )
+            )
+
+    def along_x(_):
+        total = z_sum[y]
+        for j, copy in enumerate(rsy):
+            copy.wait_recv()
+            total = total + y_recv[j].astype(F32)
+        x_all[x] = total.astype(BF16)
+        for j, peer in enumerate(x_peers):
+            rsx.append(
+                send(
+                    x_all.at[x], x_all.at[x], rsx_send_sem.at[j], rsx_recv_sem.at[j],
+                    {"dp": peer},
+                )
+            )
+
+    def last_sum(_):
+        for copy in rsx:
+            copy.wait_recv()
+        for parity in range(2):
+            total = x_all[parity].astype(F32)
+            for j in range(parity + 2, n_x, 2):
+                total = total + x_all[j].astype(F32)
+            wgrad[:, pl.ds(parity * half, half)] = total * (1.0 / norm)
+        store(wgrad, wgrad_hbm)
+
+    def keep(_):
+        for t in range(2):
+            store(attn.at[pl.ds(t * HALF, HALF)], attn_hbm.at[token_rows(t)])
+        store(w, w_hbm)
+
+    def grad_sum(t):
+        store(dq.at[t], dq_hbm.at[token_rows(t)])
+        for copy, slot in grads:
+            if slot == t:
+                copy.wait()
+        for own, got, out, hbm in (
+            (dk_own, dk_recv, dk_send, dk_hbm), (dv_own, dv_recv, dv_send, dv_hbm)
+        ):
+            def add_rows(i, carry, own=own, got=got, out=out):
+                rows = pl.ds(pl.multiple_of(i * 32, 32), 32)
+                out[t, rows] = (own[t, rows] + got[t, rows].astype(F32)).astype(BF16)
+                return carry
+
+            lax.fori_loop(0, HALF // 32, add_rows, 0)
+            store(out.at[t], hbm.at[token_rows(t)])
+
     plan = PLAN if n_z == 8 else SMALL_PLAN
     steps = {
         "ag": ag_step, "f0": functools.partial(forward, 0), "f1": functools.partial(forward, 1),
         "wg": weight_rows, "xs": aside_level, "zs": chain_level, "ga": grad_attn,
         "b0": functools.partial(backward, 0), "b1": functools.partial(backward, 1),
+        "ys": along_y, "yx": along_x, "xx": last_sum, "kp": keep, "gs": grad_sum,
     }
     for item in " ".join(plan).split():
         steps[item[:2]](int(item[2:]))
-
-    stores = []
-
-    def store(src, dst):
-        copy = pltpu.make_async_copy(src, dst, store_sem.at[len(stores)])
-        copy.start()
-        stores.append(copy)
-
-    rsy = [
-        send(
-            y_send.at[(y + j) % n_y], y_recv.at[j - 1], rsy_send_sem.at[j - 1],
-            rsy_recv_sem.at[j - 1], {"seq": peer},
-        )
-        for j, peer in enumerate(y_peers, 1)
-    ]
-    for t in range(2):
-        store(dq.at[t], dq_hbm.at[token_rows(t)])
-
-    tiles = width // HALF
-
-    def layer_tile(i, carry):
-        cols = pl.ds(pl.multiple_of(i * HALF, HALF), HALF)
-        right = w[:, :, :, cols].reshape(hd, HALF)
-        layer[:, cols] = dot(attn[...], right, ((1,), (0,))).astype(BF16)
-        return carry
-
-    lax.fori_loop(0, tiles // 2, layer_tile, 0)
-
-    total = z_sum[y]
-    for j, copy in enumerate(rsy):
-        copy.wait_recv()
-        total = total + y_recv[j].astype(F32)
-    x_all[x] = total.astype(BF16)
-    rsx = [
-        send(
-            x_all.at[x], x_all.at[x], rsx_send_sem.at[j], rsx_recv_sem.at[j], {"dp": peer}
-        )
-        for j, peer in enumerate(x_peers)
-    ]
-    lax.fori_loop(tiles // 2, tiles, layer_tile, 0)
-    for t in range(2):
-        store(layer.at[pl.ds(t * HALF, HALF)], layer_hbm.at[token_rows(t)])
-
-    grads_of = {t: [copy for copy, slot in grads if slot == t] for t in range(2)}
-    for t in (0, 1):
-        for copy in grads_of[t]:
-            copy.wait()
-        for own, got, out, hbm in (
-            (dk_own, dk_recv, dk_send, dk_hbm), (dv_own, dv_recv, dv_send, dv_hbm)
-        ):
-            def add_rows(i, carry, own=own, got=got, out=out, t=t):
-                rows = pl.ds(pl.multiple_of(i * 32, 32), 32)
-                out[t, rows] = (own[t, rows] + got[t, rows].astype(F32)).astype(BF16)
-                return carry
-
-            lax.fori_loop(0, HALF // 32, add_rows, 0)
-            store(out.at[t], hbm.at[token_rows(t)])
-
-    for copy in rsx:
-        copy.wait_recv()
-    for parity in range(2):
-        total = x_all[parity].astype(F32)
-        for j in range(parity + 2, n_x, 2):
-            total = total + x_all[j].astype(F32)
-        wgrad[:, pl.ds(parity * half, half)] = total * (1.0 / norm)
-    store(wgrad, wgrad_hbm)
 
     waited = [copy for copy, _ in grads]
     for copy in sent:
         if not any(copy is other for other in waited):
             copy.wait_send()
+    for copy in stores:
+        copy.wait()
+
+
+def layer_kernel(
+    attn_hbm, w_hbm, dq_in, dk_in, dv_in, wgrad_in,
+    layer_hbm, dq_out, dk_out, dv_out, wgrad_out,
+    attn, w, layer, dq, dk, dv, wgrad,
+    load_sem, store_sem, in_sem, out_sem,
+):
+    hd, width = attn.shape[1], layer.shape[1]
+    size = width // LAYER_PARTS
+    parts = [pl.ds(n * size, size) for n in range(LAYER_PARTS)]
+    loads = [pltpu.make_async_copy(attn_hbm, attn, load_sem.at[LAYER_PARTS])]
+    for n, cols in enumerate(parts):
+        loads.append(
+            pltpu.make_async_copy(
+                w_hbm.at[:, :, :, cols], w.at[:, :, :, cols], load_sem.at[n]
+            )
+        )
+    moved = (
+        (dq_in, dq, dq_out), (dk_in, dk, dk_out), (dv_in, dv, dv_out), (wgrad_in, wgrad, wgrad_out)
+    )
+    moves = [
+        pltpu.make_async_copy(source, held, in_sem.at[n])
+        for n, (source, held, _) in enumerate(moved)
+    ]
+    for copy in loads + moves:
+        copy.start()
+    stores = []
+    loads[0].wait()
+    for n, cols in enumerate(parts):
+        loads[n + 1].wait()
+        right = w[:, :, :, cols].reshape(hd, size)
+        layer[:, cols] = dot(attn[...], right, ((1,), (0,))).astype(BF16)
+        stores.append(
+            pltpu.make_async_copy(layer.at[:, cols], layer_hbm.at[:, cols], store_sem.at[n])
+        )
+        stores[-1].start()
+        if n < len(moved):
+            _, held, target = moved[n]
+            moves[n].wait()
+            stores.append(pltpu.make_async_copy(held, target, out_sem.at[n]))
+            stores[-1].start()
     for copy in stores:
         copy.wait()
 
@@ -515,7 +558,6 @@
         vmem((2, HALF, hd), BF16),
         vmem((2, HALF, hd), BF16),
         vmem((2, HALF, hd), BF16),
-        vmem((2 * HALF, width), BF16),
         vmem((n_zy, CORES, 16, width), BF16),
         vmem((n_zy, 16, width), BF16),
         vmem((n_z, 2, n_y, 16, width // 4), BF16),
@@ -530,7 +572,7 @@
         vmem((n_x, 16, width // 2), BF16),
         vmem((16, width), F32),
         dma((9,)),
-        dma((9,)),
+        dma((10,)),
         dma((2 * n_z,)), dma((2 * n_z,)),
         dma((n_y - 1,)), dma((n_y - 1,)),
         dma((n_plus,)), dma((n_plus,)),
@@ -547,17 +589,18 @@
     ]
     hbm = pl.BlockSpec(memory_space=pl.ANY)
     smem = pl.BlockSpec(memory_space=pltpu.SMEM)
-    layer_out, grad_query, grad_keys, grad_values, weight_grad = pl.pallas_call(
+    attn, weight, *grads = pl.pallas_call(
         functools.partial(kernel, sizes),
         out_shape=(
-            jax.ShapeDtypeStruct((rows, width), BF16),
+            jax.ShapeDtypeStruct((rows, hd), BF16),
+            jax.ShapeDtypeStruct((n_zy, CORES, 16, width), BF16),
             jax.ShapeDtypeStruct((rows, hd), BF16),
             jax.ShapeDtypeStruct((rows, hd), BF16),
             jax.ShapeDtypeStruct((rows, hd), BF16),
             jax.ShapeDtypeStruct((16, width), F32),
         ),
         in_specs=[hbm] * 5 + [smem] * 2,
-        out_specs=(hbm,) * 5,
+        out_specs=(hbm,) * 6,
         scratch_shapes=scratch,
         compiler_params=pltpu.CompilerParams(
             collective_id=0, has_side_effects=True, vmem_limit_bytes=60 * 1024 * 1024
@@ -565,7 +608,25 @@
     )(
         queries[0], memory_keys[0], memory_values[0], out_weight, grad_out[0], key_first, key_last
     )
-    return (layer_out[None], grad_query[None], grad_keys[None], grad_values[None], weight_grad)
+    layer_out, *grads = pl.pallas_call(
+        layer_kernel,
+        out_shape=(
+            jax.ShapeDtypeStruct((rows, width), BF16),
+            *(jax.ShapeDtypeStruct(grad.shape, grad.dtype) for grad in grads),
+        ),
+        in_specs=[hbm] * 6,
+        out_specs=(hbm,) * 5,
+        scratch_shapes=[
+            vmem((rows, hd), BF16),
+            vmem((n_zy, CORES, 16, width), BF16),
+            vmem((rows, width), BF16),
+            *(vmem(grad.shape, grad.dtype) for grad in grads),
+            dma((LAYER_PARTS + 1,)), dma((LAYER_PARTS,)), dma((4,)), dma((4,)),
+        ],
+        compiler_params=pltpu.CompilerParams(vmem_limit_bytes=60 * 1024 * 1024),
+    )(attn, weight, *grads)
+    weight_grad = grads.pop()
+    return (layer_out[None], *(grad[None] for grad in grads), weight_grad)
 
 
 def solution(mesh, n_y=Y_CHIPS):

time: 87.8 us -> 80.4 us (0.916)
  local copies, waits for them, and re-layouts: 6.89 us -> 0 us
  Pallas kernels: 80.2 us -> 79.3 us
    unnamed x13 -> x0, local copies, waits for them, and re-layouts: 6.89 us -> none
    pallas_call x1, Pallas kernels: 80.2 us -> 73.6 us  [body(): pl.pallas_call(functools.partial(kernel, sizes), out_shape=(jax.ShapeDtyp...]
    pallas_call x0 -> x1, Pallas kernels: none -> 5.69 us  [body(): pl.pallas_call(layer_kernel, out_shape=(jax.ShapeDtypeStruct((rows, width...]
where the time goes in v4:
time: 80.4 us; the launch traced here: 80.1 us
  Pallas kernels  79.3 us (99%)
  between operations  0.82 us (1%)
    pallas_call x1, Pallas kernels, body(): pl.pallas_call(functools.partial(kernel, sizes), out_shape=(jax.ShapeDtyp...  73.6 us
    pallas_call x1, Pallas kernels, body(): pl.pallas_call(layer_kernel, out_shape=(jax.ShapeDtypeStruct((rows, width...  5.69 us

profile of v4, /device:TPU:1, one launch (start us, length us, event | category | flops | bytes accessed | tf_op | source)
XLA Modules:
  0.0 80.1 jit_solution(14027793385521306919)
XLA Ops:
  0.6 73.6 %shard_map.110 = (bf16[512,1024]{1,0:T(8,128)(2,1)}, bf16[32,2,16,2048]{3,2,1,0:T(8,128)(2,1)}, bf16[512,1024]{1,0:T(8,128)(2,1)}, bf16[512,1024]{1,0:T(8,128)(2...) custom-call(bf16[512,1024]{1,0:T(8,128)(2,1)} %bitcast.9, bf16[512,1024]{1,0:T(8,128)(2,1)} %bitcast.10, ...), custom_call_target="tpu_custom_call" | custom-call | tf_op jit(solution)/shard_map/pallas_call | solution.py:592
  74.3 5.7 %shard_map.111 = (bf16[512,2048]{1,0:T(8,128)(2,1)}, bf16[512,1024]{1,0:T(8,128)(2,1)}, bf16[512,1024]{1,0:T(8,128)(2,1)}, bf16[512,1024]{1,0:T(8,128)(2,1)}, f32[16,2048]{1,0:T(8,128)}) custom-call(bf16[512,1024]{1,0:T(8,128)(2,1)} %get-tuple-element.16.attn_hbm, bf16[32,2,16,2048]{3,2,1,0:T(8,128)(2,1)} %get-tuple-element.17.w_hbm, ...), custom_call_target="tpu_custom_call" | custom-call | tf_op jit(solution)/shard_map/pallas_call | solution.py:611

commit v5 on v4

--- a/solution.py
+++ b/solution.py
@@ -18,13 +18,13 @@
 NEVER = -1e30
 LAYER_PARTS = 4
 PLAN = (
-    "ag0 f00 f01 f10", "wg0 ag1 f11 f02", "wg1 xs0 f03 f12", "ag2 wg2 xs1 zs4",
-    "f13 wg3 xs2 ag3", "ga0 zs3 b10 xs3", "b00 zs2 ag4 ga1", "b11 b01 zs1 ga2",
-    "b12 b02 ag5 zs0", "ys0 ga3 kp0 b13", "yx0 b03 xx0 gs0", "gs1",
+    "hs1 ag0 f00 hs2", "f01 f10 wg0 hs3", "ag1 f11 f02 wg1", "xs0 f03 ag2 f12",
+    "wg2 xs1 zs4 f13", "wg3 xs2 ag3 ga0", "zs3 b10 xs3 b00", "zs2 ag4 ga1 b11",
+    "b01 zs1 ga2 b12", "b02 ag5 zs0 ys0", "ga3 kp0 b13 yx0", "b03 xx0 gs0 gs1",
 )
 SMALL_PLAN = (
-    "ag0 f00 f10 wg0", "ag1 f01 xs0 ag2", "f11 wg1 ga0 zs2", "xs1 b10 b00 zs1",
-    "ag3 ga1 kp0 b11", "zs0 ys0 b01 yx0", "gs0 gs1 xx0",
+    "ag0 hs1 f00 f10", "wg0 ag1 f01 xs0", "ag2 f11 wg1 ga0", "zs2 xs1 b10 b00",
+    "zs1 ag3 ga1 kp0", "b11 zs0 ys0 b01", "yx0 gs0 gs1 xx0",
 )
 
 
@@ -144,21 +144,25 @@
         return pl.ds(pl.multiple_of(r * HALF, HALF), HALF)
 
     halo = {}
-    for t in (1, 0):
-        partner_far = near_first(partners[t] // CORES // n_y)[::-1]
-        for i, r in enumerate(partner_far):
-            halo[t, i] = []
-            for which, (src, dst) in enumerate(((k_hbm, kg), (v_hbm, vg))):
-                n = (t * pairs + i) * 2 + which
-                halo[t, i].append(
-                    send(
-                        src.at[token_rows(t), pair_cols(r)],
-                        dst.at[t, pl.ds(HALF, HALF), pair_cols(r)],
-                        halo_send_sem.at[n],
-                        halo_recv_sem.at[n],
-                        {"seq": partners[t]},
-                    )
+
+    def share_keys(t, i):
+        r = near_first(partners[t] // CORES // n_y)[::-1][i]
+        halo[t, i] = []
+        for which, (src, dst) in enumerate(((k_hbm, kg), (v_hbm, vg))):
+            n = (t * pairs + i) * 2 + which
+            halo[t, i].append(
+                send(
+                    src.at[token_rows(t), pair_cols(r)],
+                    dst.at[t, pl.ds(HALF, HALF), pair_cols(r)],
+                    halo_send_sem.at[n],
+                    halo_recv_sem.at[n],
+                    {"seq": partners[t]},
                 )
+            )
+
+    share_keys(1, 0)
+    for i in range(pairs):
+        share_keys(0, i)
 
     def slab(z_index, start, size):
         return w.at[pl.ds(z_index * n_y, n_y), c, :, wide(start, size)]
@@ -469,6 +473,7 @@
 
     plan = PLAN if n_z == 8 else SMALL_PLAN
     steps = {
+        "hs": functools.partial(share_keys, 1),
         "ag": ag_step, "f0": functools.partial(forward, 0), "f1": functools.partial(forward, 1),
         "wg": weight_rows, "xs": aside_level, "zs": chain_level, "ga": grad_attn,
         "b0": functools.partial(backward, 0), "b1": functools.partial(backward, 1),

time: 80.4 us -> 76.7 us (0.954)
  Pallas kernels: 79.3 us -> 75.8 us
    pallas_call x1, Pallas kernels: 73.6 us -> 70.1 us  [body(): pl.pallas_call(functools.partial(kernel, sizes), out_shape=(jax.ShapeDtyp...]
where the time goes in v5:
time: 76.7 us; the launch traced here: 76.6 us
  Pallas kernels  75.8 us (99%)
  between operations  0.82 us (1%)
    pallas_call x1, Pallas kernels, body(): pl.pallas_call(functools.partial(kernel, sizes), out_shape=(jax.ShapeDtyp...  70.1 us
    pallas_call x1, Pallas kernels, body(): pl.pallas_call(layer_kernel, out_shape=(jax.ShapeDtypeStruct((rows, width...  5.69 us

profile of v5, /device:TPU:1, one launch (start us, length us, event | category | flops | bytes accessed | tf_op | source)
XLA Modules:
  0.0 76.6 jit_solution(15891414535933145280)
XLA Ops:
  0.6 70.1 %shard_map.110 = (bf16[512,1024]{1,0:T(8,128)(2,1)}, bf16[32,2,16,2048]{3,2,1,0:T(8,128)(2,1)}, bf16[512,1024]{1,0:T(8,128)(2,1)}, bf16[512,1024]{1,0:T(8,128)(2...) custom-call(bf16[512,1024]{1,0:T(8,128)(2,1)} %bitcast.9, bf16[512,1024]{1,0:T(8,128)(2,1)} %bitcast.10, ...), custom_call_target="tpu_custom_call" | custom-call | tf_op jit(solution)/shard_map/pallas_call | solution.py:597
  70.8 5.7 %shard_map.111 = (bf16[512,2048]{1,0:T(8,128)(2,1)}, bf16[512,1024]{1,0:T(8,128)(2,1)}, bf16[512,1024]{1,0:T(8,128)(2,1)}, bf16[512,1024]{1,0:T(8,128)(2,1)}, f32[16,2048]{1,0:T(8,128)}) custom-call(bf16[512,1024]{1,0:T(8,128)(2,1)} %get-tuple-element.16.attn_hbm, bf16[32,2,16,2048]{3,2,1,0:T(8,128)(2,1)} %get-tuple-element.17.w_hbm, ...), custom_call_target="tpu_custom_call" | custom-call | tf_op jit(solution)/shard_map/pallas_call | solution.py:616

commit v6 on v5

--- a/solution.py
+++ b/solution.py
@@ -18,9 +18,9 @@
 NEVER = -1e30
 LAYER_PARTS = 4
 PLAN = (
-    "hs1 ag0 f00 hs2", "f01 f10 wg0 hs3", "ag1 f11 f02 wg1", "xs0 f03 ag2 f12",
-    "wg2 xs1 zs4 f13", "wg3 xs2 ag3 ga0", "zs3 b10 xs3 b00", "zs2 ag4 ga1 b11",
-    "b01 zs1 ga2 b12", "b02 ag5 zs0 ys0", "ga3 kp0 b13 yx0", "b03 xx0 gs0 gs1",
+    "hs1 ag0 f00 hs2", "f01 f10 wg0 hs3", "ag1 f11 wg1 f02", "xs0 f03 ag2 f12",
+    "wg2 xs1 zs4 f13", "wg3 xs2 ag3 zs3", "xs3 ga0 b10 b00", "zs2 ag4 ga1 b11",
+    "b01 zs1 ga2 b12", "ag5 b02 zs0 ys0", "ga3 kp0 b13 b03", "yx0 gs0 xx0 gs1",
 )
 SMALL_PLAN = (
     "ag0 hs1 f00 f10", "wg0 ag1 f01 xs0", "ag2 f11 wg1 ga0", "zs2 xs1 b10 b00",
@@ -51,6 +51,7 @@
 ):
     n_seq, n_x, n_y, n_z, n_plus, n_minus, heads, width, norm = sizes
     scale = 1.0 / math.sqrt(HDIM)
+    log_scale = scale * math.log2(math.e)
     s = lax.axis_index("seq")
     x = lax.axis_index("dp")
     c = s % CORES
@@ -248,9 +249,9 @@
             copy.wait_recv()
         for h in (2 * far[i], 2 * far[i] + 1):
             cols = wide(h * HDIM, HDIM)
-            scores = dot(kg[t, :, cols], q[t, :, cols], ((1,), (1,))) * scale + bias[t]
+            scores = dot(kg[t, :, cols], q[t, :, cols], ((1,), (1,))) * log_scale + bias[t]
             highest = jnp.max(scores, axis=0, keepdims=True)
-            raised = jnp.exp(scores - highest)
+            raised = jnp.exp2(scores - highest)
             total = jnp.sum(raised, axis=0, keepdims=True)
             p = raised * (1.0 / total)
             probs[t, h] = p

time: 76.7 us -> 76.2 us (level)
  no operation moved by 1% of the time
where the time goes in v6:
time: 76.2 us
  Pallas kernels  75.3 us (99%)
  between operations  0.82 us (1%)
    pallas_call x1, Pallas kernels, body(): pl.pallas_call(functools.partial(kernel, sizes), out_shape=(jax.ShapeDtyp...  69.6 us
    pallas_call x1, Pallas kernels, body(): pl.pallas_call(layer_kernel, out_shape=(jax.ShapeDtypeStruct((rows, width...  5.69 us

profile of v6, /device:TPU:1, one launch (start us, length us, event | category | flops | bytes accessed | tf_op | source)
XLA Modules:
  0.0 76.2 jit_solution(14638343278485285869)
XLA Ops:
  0.6 69.6 %shard_map.110 = (bf16[512,1024]{1,0:T(8,128)(2,1)}, bf16[32,2,16,2048]{3,2,1,0:T(8,128)(2,1)}, bf16[512,1024]{1,0:T(8,128)(2,1)}, bf16[512,1024]{1,0:T(8,128)(2...) custom-call(bf16[512,1024]{1,0:T(8,128)(2,1)} %bitcast.9, bf16[512,1024]{1,0:T(8,128)(2,1)} %bitcast.10, ...), custom_call_target="tpu_custom_call" | custom-call | tf_op jit(solution)/shard_map/pallas_call | solution.py:598
  70.3 5.7 %shard_map.111 = (bf16[512,2048]{1,0:T(8,128)(2,1)}, bf16[512,1024]{1,0:T(8,128)(2,1)}, bf16[512,1024]{1,0:T(8,128)(2,1)}, bf16[512,1024]{1,0:T(8,128)(2,1)}, f32[16,2048]{1,0:T(8,128)}) custom-call(bf16[512,1024]{1,0:T(8,128)(2,1)} %get-tuple-element.16.attn_hbm, bf16[32,2,16,2048]{3,2,1,0:T(8,128)(2,1)} %get-tuple-element.17.w_hbm, ...), custom_call_target="tpu_custom_call" | custom-call | tf_op jit(solution)/shard_map/pallas_call | solution.py:617
